TPU v7x, 512 devices: a whole 4x4x16 slice. The times are simulated.
512 devices in a mesh: blk: 16 (over y, z_hi, core), act: 32 (over x, z_lo).
Axes of the slice: x: 4, y: 4, z: 16 (z_hi: 2, z_lo: 8; z = z_hi * 8 + z_lo), core: 2. Of those that a mesh axis runs over, the one named last changes fastest.
Arguments:
- star_state: float32 [12, 131072], P(None, 'blk'), may hold values from -4 to 4
- star_mass: float32 [131072], P('blk'), may hold values from 0.1 to 10
- star_level: int32 [131072], P('blk'), may hold values from 0 to 3, as said below
- active_slots: int32 [32768], P('act'), may hold values from -1 to 131071, as said below
Outputs:
- advanced: float32 [12, 32768], P(None, 'act')
Inputs may be any that keep to these rules, and one draw needn't show every extreme that they name: `active_slots`: the indices of the level-2 stars, then -1 up to the next multiple of 128 slots, then the indices of the level-3 stars, then -1 to the end. Each of the two lists holds one star or more, both together exactly 13312; every star of level 2 or 3 appears once and no other star appears. `star_level`: exactly 13312 stars have level 2 or 3: those listed in active_slots.
All inputs are finite; a program needn't handle non-finite values.
Results may differ from a plain program's by a relative error of at most 0.0003.
Values sent between devices are 32-bit elements; how exact they have to be, the bound alone decides.
No kernel may reach another device: no remote copies, remote signals or barrier semaphores. Data moves between devices by JAX's collectives and lax.ppermute only.
A program may use at most 64 MiB of HBM per device.

v0:
```python
import math

import jax
import jax.numpy as jnp
from jax import lax
from jax.sharding import PartitionSpec as P

SOFTENING = 0.0025
ONE_THIRD = 1.0 / 3.0
ONE_TWELFTH = 1.0 / 12.0


def since_update(level_value):
    return jnp.where(
        level_value == 0,
        0.375,
        jnp.where(level_value == 1, 0.125, jnp.where(level_value == 2, 0.125, 0.0625)),
    ).astype(jnp.float32)


def predict(star_rows, elapsed_time):
    position = star_rows[0:3]
    velocity = star_rows[3:6]
    accel_old = star_rows[6:9]
    jerk_old = star_rows[9:12]
    new_place = position + elapsed_time * (
        velocity + elapsed_time * 0.5 * (accel_old + elapsed_time * ONE_THIRD * jerk_old)
    )
    new_speed = velocity + elapsed_time * (accel_old + elapsed_time * 0.5 * jerk_old)
    return jnp.concatenate([new_place, new_speed], 0)


def pair_block(targets, sources, weights):
    offset = sources[0:3, None, :] - targets[0:3, :, None]
    relative = sources[3:6, None, :] - targets[3:6, :, None]
    radius_sq = jnp.sum(offset * offset, 0) + SOFTENING
    inverse = 1.0 / jnp.sqrt(radius_sq)
    inverse_sq = inverse * inverse
    strength = weights[None, :] * inverse * inverse_sq
    approach = jnp.sum(offset * relative, 0) * inverse_sq
    new_accel = jnp.sum(strength * offset, 2)
    new_jerk = jnp.sum(strength * (relative - 3.0 * approach * offset), 2)
    return jnp.concatenate([new_accel, new_jerk], 0)


def pair_sum(targets, sources, weights):
    source_count = sources.shape[1]
    target_count = targets.shape[1]
    wanted = min(4096, max(1024, 524288 // target_count))
    block_size = math.gcd(source_count, wanted)
    block_count = source_count // block_size

    def add_part(turn, running):
        first_index = (turn * block_size).astype(jnp.int32)
        source_part = lax.dynamic_slice_in_dim(sources, first_index, block_size, 1)
        weight_part = lax.dynamic_slice_in_dim(weights, first_index, block_size, 0)
        return running + pair_block(targets, source_part, weight_part)

    return lax.fori_loop(0, block_count, add_part, jnp.zeros((6, target_count), jnp.float32))


def tile_forces(targets, live_rows, sources, weights):
    target_count = targets.shape[1]
    tile_size = math.gcd(target_count, 512)
    tile_count = target_count // tile_size
    target_tiles = targets.reshape(6, tile_count, tile_size).transpose(1, 0, 2)
    live_tiles = live_rows.reshape(tile_count, tile_size)

    def tile_force(tile_args):
        tile_rows, tile_live = tile_args
        return lax.cond(
            jnp.any(tile_live),
            lambda: pair_sum(tile_rows, sources, weights),
            lambda: jnp.zeros((6, tile_size), jnp.float32),
        )

    result = lax.map(tile_force, (target_tiles, live_tiles))
    return result.transpose(1, 0, 2).reshape(6, target_count)


def correct(previous, forces, elapsed_time):
    position = previous[0:3]
    velocity = previous[3:6]
    accel_old = previous[6:9]
    jerk_old = previous[9:12]
    new_accel = forces[0:3]
    new_jerk = forces[3:6]
    half_step = 0.5 * elapsed_time
    step_sq = elapsed_time * elapsed_time * ONE_TWELFTH
    new_velocity = velocity + half_step * (accel_old + new_accel) + step_sq * (jerk_old - new_jerk)
    new_position = (
        position + half_step * (velocity + new_velocity) + step_sq * (accel_old - new_accel)
    )
    return jnp.concatenate([new_position, new_velocity, new_accel, new_jerk], 0)


def local(star_state, star_mass, star_level, active_slots):
    shard_size = star_state.shape[1]
    blk_count = lax.axis_size("blk")
    blk_pos = lax.axis_index("blk")
    elapsed_time = since_update(star_level)
    shard_pred = predict(star_state, elapsed_time)
    weights = star_mass / float(shard_size * blk_count)
    source_table = jnp.concatenate([shard_pred, weights[None, :]], 0)
    target_count = active_slots.shape[0]
    live_rows = active_slots >= 0
    local_index = active_slots - blk_pos * shard_size
    owned_here = live_rows & (local_index >= 0) & (local_index < shard_size)
    clipped = jnp.clip(local_index, 0, shard_size - 1)
    picked = jnp.concatenate(
        [
            jnp.take(star_state, clipped, axis=1),
            jnp.take(star_level, clipped).astype(jnp.float32)[None, :],
        ],
        0,
    )
    packed = jnp.where(owned_here[None, :], picked, 0.0)
    fetched = lax.psum(packed, "blk")
    previous = fetched[0:12]
    slot_elapsed = since_update(fetched[12])
    targets = predict(previous, slot_elapsed)
    share_size = target_count // blk_count
    share_rows = lax.dynamic_slice_in_dim(targets, blk_pos * share_size, share_size, 1)
    share_live = lax.dynamic_slice_in_dim(live_rows, blk_pos * share_size, share_size, 0)
    source_piece = lax.all_gather(source_table, "blk", axis=1, tiled=True)
    share_forces = tile_forces(share_rows, share_live, source_piece[0:6], source_piece[6])
    forces = lax.all_gather(share_forces, "blk", axis=1, tiled=True)
    result = correct(previous, forces, slot_elapsed)
    return jnp.where(live_rows[None, :], result, 0.0)


def solution(mesh):
    placed = (P(None, "blk"), P("blk"), P("blk"), P("act"))
    return jax.shard_map(
        local, mesh=mesh, in_specs=placed, out_specs=P(None, "act"), check_vma=False
    )
```

profile of v0, /device:TPU:417, one launch (start us, length us, event | category | flops | bytes accessed | tf_op | source)
XLA Modules:
  0.0 381.2 jit_solution(11515155653696216331)
XLA Ops:
  8.1 1.5 multiply_add_fusion.1
  10.4 3.6 copy.19
  14.0 6.2 %gather_fusion.1 = s32[1024]{0:T(1024)S(1)} fusion(s32[8192]{0:T(1024)S(1)} %copy-done, s32[1024]{0:T(1024)S(1)} %fusion.7), kind=kCustom, calls=%fused_computation.1 | custom fusion | bytes 12288 | tf_op jit(solution)/shard_map/jit(_take)/gather | solution.py:113
  20.2 5.0 %gather_fusion = f32[1024,12]{1,0:T(8,128)S(1)} fusion(f32[12,8192]{0,1:T(8,128)} %copy.19, s32[1024]{0:T(1024)S(1)} %fusion.7), kind=kCustom, calls=%fused_computation | custom fusion | bytes 102400 | tf_op jit(solution)/shard_map/jit(_take)/gather | solution.py:112
  27.0 133.7 %psum.7 = f32[13,1024]{1,0:T(8,128)S(1)} all-reduce(f32[13,1024]{1,0:T(8,128)S(1)} %maximum_select_fusion), channel_id=1, replica_groups=mesh['blk'=16,'act'=32] {'blk'}, use_global_device_ids=true, to_apply=%region_0.1 | all-reduce | flops 13312 | bytes 106496 | tf_op jit(solution)/shard_map/psum | solution.py:118
  160.8 156.3 %conditional.1 = (f32[6,64]{1,0:T(8,128)}) conditional(s32[]{:T(128)} %convert_element_type.13, () %tuple.30, (f32[7,131072]{1,0:T(8,128)}, f32[6,1024]{1,0:T(8,128)S(1)}, s32[]{:T(128)}) %tuple.31), branch_computations={%region_2.3_spmd, %region_3.10_spmd} | conditional | flops 12059400 | bytes 9895193 | solution.py:71
  160.8 2.7 slice.69
  163.6 153.5 %while.19 = (s32[]{:T(128)}, f32[6,64]{1,0:T(8,128)}, f32[6,131072]{1,0:T(8,128)}, f32[6,64]{1,0:T(8,128)S(1)}, f32[131072]{0:T(1024)S(1)}, /*index=5*/s32[]{:T(128)}, s32[]{:T(128)}, s32[]{}, s32[]{:T(128)}, s32[]{:T(128)}) while((s32[]{:T(128)}, f32[6,64]{1,0:T(8,128)}, f32[6,131072]{1,0:T(8,128)}, f32[6,64]{1,0:T(8,128)S(1)}, ...), condition=%wide.region_9.9_spmd.clone, body=%wide.region_4.8_spmd.clone.sunk | while | flops 12059400 | bytes 8843445 | solution.py:59
  165.9 1.3 fusion.18
  170.0 1.3 fusion.18
  171.3 1.3 maximum_add_fusion.2
  174.9 1.3 fusion.18
  176.1 1.3 maximum_add_fusion.2
  179.7 1.3 fusion.18
  180.9 1.3 maximum_add_fusion.2
  184.5 1.3 fusion.18
  185.7 1.3 maximum_add_fusion.2
  189.3 1.3 fusion.18
  190.6 1.3 maximum_add_fusion.2
  194.1 1.3 fusion.18
  195.4 1.3 maximum_add_fusion.2
  198.9 1.3 fusion.18
  200.2 1.3 maximum_add_fusion.2
  203.8 1.3 fusion.18
  205.0 1.3 maximum_add_fusion.2
  208.6 1.3 fusion.18
  209.8 1.3 maximum_add_fusion.2
  214.7 1.3 maximum_add_fusion.2
  218.2 1.3 fusion.18
  219.5 1.3 maximum_add_fusion.2
  223.0 1.3 fusion.18
  224.3 1.3 maximum_add_fusion.2
  229.1 1.3 maximum_add_fusion.2
  232.7 1.3 fusion.18
  233.9 1.3 maximum_add_fusion.2
  238.7 1.3 maximum_add_fusion.2
  242.3 1.3 fusion.18
  243.6 1.3 maximum_add_fusion.2
  247.1 1.3 fusion.18
  248.4 1.3 maximum_add_fusion.2
  251.9 1.3 fusion.18
  253.2 1.3 maximum_add_fusion.2
  256.8 1.3 fusion.18
  258.0 1.3 maximum_add_fusion.2
  262.8 1.3 maximum_add_fusion.2
  266.4 1.3 fusion.18
  267.6 1.3 maximum_add_fusion.2
  272.5 1.3 maximum_add_fusion.2
  276.0 1.3 fusion.18
  277.3 1.3 maximum_add_fusion.2
  280.8 1.3 fusion.18
  282.1 1.3 maximum_add_fusion.2
  286.9 1.3 maximum_add_fusion.2
  290.5 1.3 fusion.18
  291.7 1.3 maximum_add_fusion.2
  296.5 1.3 maximum_add_fusion.2
  300.1 1.3 fusion.18
  301.4 1.3 maximum_add_fusion.2
  306.2 1.3 maximum_add_fusion.2
  309.7 1.3 fusion.18
  311.0 1.3 maximum_add_fusion.2
  314.6 1.3 fusion.18
  315.8 1.3 maximum_add_fusion.2
  317.1 56.5 %all-gather = f32[16,64,6]{1,2,0:T(8,128)S(1)} all-gather(f32[1,64,6]{1,2,0:T(8,128)} %bitcast.8), channel_id=1, replica_groups=mesh['blk'=16,'act'=32] {'blk'}, dimensions={0}, use_global_device_ids=true | all-gather | bytes 26112 | tf_op jit(solution)/shard_map/all_gather | solution.py:127
  (196 shorter events, 86.6 us)
Async XLA Ops:
  6.5 154.3 %all-gather.3.cloned.1.call-start = ((), (), s32[]{:S(2)}) async-start(), calls=%async_computation | async-start | bytes 4456448 | tf_op jit(solution)/shard_map/all_gather | solution.py:125
  8.1 5.9 %copy-start.1 = (s32[1024]{0:T(1024)S(1)}, s32[1024]{0:T(1024)}, u32[]{:S(2)}) copy-start(s32[1024]{0:T(1024)} %param.11) | copy-start | bytes 12292
  8.1 5.9 %copy-start = (s32[8192]{0:T(1024)S(1)}, s32[8192]{0:T(1024)}, u32[]{:S(2)}) copy-start(s32[8192]{0:T(1024)} %param.10) | copy-start | bytes 98308
Sparse Core Ops, SparseCore 0:
  10.6 116.8 all-gather.2
where the time goes:
time: 383 us; the launch traced here: 381 us
  blocking collectives  190 us (50%)
  other arithmetic  123 us (32%)
  local copies, waits for them, and re-layouts  52.6 us (14%)
  between operations  14.1 us (4%)
    psum x1, blocking collectives, local(): fetched = lax.psum(packed, 'blk')  134 us
    all_gather x1, blocking collectives, local(): forces = lax.all_gather(share_forces, 'blk', axis=1, tiled=True)  56.5 us
    add x32, other arithmetic, add_part(): return running + pair_block(targets, source_part, weight_part)  40.7 us
    reduce_sum x32, other arithmetic, pair_block(): new_accel = jnp.sum(strength * offset, 2)  40 us
    slice x64, local copies, waits for them, and re-layouts, pair_block(): relative = sources[3:6, None, :] - targets[3:6, :, None]  34.5 us
    reduce_sum x32, other arithmetic, pair_block(): radius_sq = jnp.sum(offset * offset, 0) + SOFTENING  26.7 us
    mul x32, other arithmetic, pair_block(): new_jerk = jnp.sum(strength * (relative - 3.0 * approach * offset), 2)  10 us
  transfers between devices with their start and end apart: 1, of which 0 were waited for; matrix products, arithmetic and copies ran while one was open for 4% of the time, Pallas kernels for 0%

commit v1 on v0

v1 whole, which is shorter than its diff:
```python
import functools

import jax
import jax.numpy as jnp
from jax import lax
from jax.experimental import pallas as pl
from jax.experimental.pallas import tpu as pltpu
from jax.sharding import Mesh, PartitionSpec as P

SOFTENING = 0.0025
STARS = 131072
ONE_THIRD = 1.0 / 3.0
ONE_TWELFTH = 1.0 / 12.0
bf16 = jnp.bfloat16
f32 = jnp.float32
AXES = ("y", "zh", "core", "xh", "xl", "zl")
SIZES = (4, 2, 2, 2, 2, 8)
BLK = ("y", "zh", "core")
ACT = ("xh", "xl", "zl")
SHARD = 8192
HALF = 512
PART = 256
MEMBERS = 16
CHUNK = 512
SOURCES = 2 * SHARD
FULL = pl.BlockSpec(memory_space=pltpu.VMEM)
SCALARS = pl.BlockSpec(memory_space=pltpu.SMEM)
PARAMS = pltpu.CompilerParams(vmem_limit_bytes=48 * 2**20)
NN = (((1,), (0,)), ((), ()))
TN = (((0,), (0,)), ((), ()))
dot = functools.partial(lax.dot_general, preferred_element_type=f32)


def exchange_groups():
    groups = []
    for core in range(2):
        for x in range(2):
            for zl in range(8):
                groups.append(
                    [
                        (((y * 2 + zh) * 2 + core) * 4 + column) * 8 + zl
                        for y in range(4)
                        for zh in range(2)
                        for column in (x, 3 - x)
                    ]
                )
    return groups


def rows_of(value):
    return lax.broadcasted_iota(jnp.int32, value.shape, 0)


def split(value):
    high = value.astype(bf16).astype(f32)
    rest = value - high
    middle = rest.astype(bf16).astype(f32)
    return high, middle, rest - middle


def high_low(value):
    high = value.astype(bf16)
    return high, (value - high.astype(f32)).astype(bf16)


def table_kernel(state, mass, level, table):
    lev = level[...]
    dt = jnp.where(lev == 0, 0.375, jnp.where(lev == 3, 0.0625, 0.125)).astype(f32)
    x, v, a, j = state[0:3], state[3:6], state[6:9], state[9:12]
    place = x + dt * (v + dt * 0.5 * (a + dt * ONE_THIRD * j))
    speed = v + dt * (a + dt * 0.5 * j)
    step_sq = dt * dt * ONE_TWELFTH
    half = 0.5 * dt
    table[0:3, :] = place
    table[3:6, :] = speed
    table[6:7, :] = mass[...]
    table[7:8, :] = dt
    table[8:11, :] = x + half * v + step_sq * a
    table[11:14, :] = v + half * a + step_sq * j
    table[14:15, :] = jnp.sum(place * place, 0, keepdims=True)
    table[15:16, :] = 3.0 * jnp.sum(place * speed, 0, keepdims=True)


def lookup_kernel(where, slots, mine, other, out):
    first, core = where[0], where[1]
    tables = ((mine, first + core * SHARD), (other, first + (1 - core) * SHARD))
    groups = HALF // 128
    index = slots[pl.ds(core * groups, groups), :]
    picked = [(jnp.zeros((8, 128), f32),) * 2 for _ in range(groups)]
    for table, start in tables:
        local_index = index - start
        low = [jnp.broadcast_to((local_index & 127)[g : g + 1], (8, 128)) for g in range(groups)]
        high = [jnp.broadcast_to((local_index >> 7)[g : g + 1], (8, 128)) for g in range(groups)]

        def look(h, carry):
            at = pl.ds(pl.multiple_of(h * 128, 128), 128)
            tiles = (table[0:8, at], table[8:16, at])
            result = []
            for g in range(groups):
                hit = high[g] == h
                result.append(
                    tuple(
                        jnp.where(
                            hit,
                            jnp.take_along_axis(
                                tiles[k], low[g], axis=1, mode="promise_in_bounds"
                            ),
                            carry[g][k],
                        )
                        for k in range(2)
                    )
                )
            return result

        picked = lax.fori_loop(0, SHARD // 128, look, picked, unroll=4)
    for member in range(MEMBERS):
        for part in range(2):
            g = (member % 2) * 2 + part
            for k in range(2):
                out[member, 8 * k : 8 * k + 8, part * 128 : (part + 1) * 128] = picked[g][k]


def source_features(table, features, pull, swing, offset):
    def step(turn, _):
        at = pl.ds(pl.multiple_of(turn * CHUNK, CHUNK), CHUNK)
        to = pl.ds(pl.multiple_of(offset + turn * CHUNK, CHUNK), CHUNK)
        upper, lower = table[0:8, at], table[8:16, at]
        row = rows_of(upper)
        a, b, c = split(jnp.where(row == 7, 1.0, upper))
        d, e, f = split(lower)
        zero = jnp.zeros_like(a)
        pairs = ((a, a), (a, b), (b, c), (d, e), (f, zero))
        for k, pair in enumerate(pairs):
            features[16 * k : 16 * k + 16, to] = jnp.concatenate(pair, 0).astype(bf16)
        weight = upper[6:7] * (1.0 / STARS)
        moved = jnp.where(row == 7, 0.0, jnp.where(row == 6, 1.0, upper)) * weight
        placed = pltpu.roll(moved, 3, 0)
        turned = jnp.where(row == 7, weight, jnp.where((row >= 3) & (row < 6), -placed, 0.0))
        for ref, value in ((pull, moved), (swing, turned)):
            a, b, c = split(value)
            ref[0:16, to] = jnp.concatenate((a, b), 0).astype(bf16)
            ref[16:32, to] = jnp.concatenate((c, zero), 0).astype(bf16)
        return 0

    lax.fori_loop(0, SHARD // CHUNK, step, 0)


def target_features(target):
    row = rows_of(target)
    place = jnp.where(row < 3, target, 0.0)
    speed = pltpu.roll(target, 5, 0)
    place_sq = jnp.sum(place * place, 0, keepdims=True) + SOFTENING
    product = 3.0 * jnp.sum(place * speed, 0, keepdims=True)
    shifted = pltpu.roll(target, 3, 0)
    radius = jnp.where(row == 7, place_sq, -2.0 * place)
    near = jnp.where(
        row == 7,
        product,
        jnp.where(row < 3, -3.0 * speed, jnp.where(row < 6, -3.0 * shifted, 0.0)),
    )
    zero = jnp.zeros_like(target)
    result = []
    for value, own_row in ((radius, 6), (near, 7)):
        a, b, c = split(value)
        one = jnp.where(row == own_row, 1.0, 0.0)
        result.append(
            jnp.concatenate((a, b, c, a, b, a, one, one, one, zero), 0).astype(bf16)
        )
    return result


def force_kernel(received, mine, other, out, features, pull, swing, total):
    target_rows = received[0]
    for sender in range(2, MEMBERS, 2):
        target_rows = target_rows + received[sender]
    target = target_rows[0:8]
    source_features(mine, features, pull, swing, 0)
    source_features(other, features, pull, swing, SHARD)
    radius_part, near_part = target_features(target)
    total[...] = jnp.zeros_like(total)

    def step(turn, _):
        at = pl.ds(pl.multiple_of(turn * CHUNK, CHUNK), CHUNK)
        source = features[:, at]
        radius_sq = dot(source, radius_part, TN)
        product = dot(source, near_part, TN)
        inverse = lax.rsqrt(radius_sq)
        inverse_sq = inverse * inverse
        strength = inverse_sq * inverse
        turning = (product * inverse_sq) * strength
        pulls, swings = pull[:, at], swing[:, at]
        total[...] += dot(
            jnp.concatenate((pulls, pulls, swings, swings), 1),
            jnp.concatenate(high_low(strength) + high_low(turning), 0),
            NN,
        )
        return 0

    lax.fori_loop(0, SOURCES // CHUNK, step, 0, unroll=2)
    sums = total[0:8] + total[8:16] + total[16:24]
    place, speed = target[0:3], target[3:6]
    accel = sums[0:3] - place * sums[6:7]
    jerk = sums[3:6] - speed * sums[6:7] + place * sums[7:8]
    for member in range(MEMBERS):
        out[member, 0:3, :] = accel
        out[member, 3:6, :] = jerk
        out[member, 6:8, :] = target[6:8]
        out[member, 8:16, :] = target_rows[8:16]


def correct_kernel(received, out):
    for part in range(2):
        rows = received[part]
        force = rows[0:8]
        for sender in range(part + 2, MEMBERS, 2):
            force = force + received[sender, 0:8, :]
        dt = rows[7:8]
        accel, jerk = force[0:3], force[3:6]
        half = 0.5 * dt
        step_sq = dt * dt * ONE_TWELFTH
        velocity = rows[11:14] + half * accel - step_sq * jerk
        base = rows[8:11]
        position = base + half * velocity - step_sq * accel
        at = slice(part * PART, (part + 1) * PART)
        out[0:3, at] = position
        out[3:6, at] = velocity
        out[6:9, at] = accel
        out[9:12, at] = jerk


def local(star_state, star_mass, star_level, active_slots):
    core = lax.axis_index("core")
    pair = lax.axis_index("y") * 2 + lax.axis_index("zh")
    where = jnp.stack([pair * SOURCES, core]).astype(jnp.int32)
    table = pl.pallas_call(
        table_kernel,
        out_shape=jax.ShapeDtypeStruct((16, SHARD), f32),
        in_specs=[FULL] * 3,
        out_specs=FULL,
        compiler_params=PARAMS,
        name="table",
    )(star_state, star_mass.reshape(1, SHARD), star_level.reshape(1, SHARD))
    other = lax.ppermute(table, "core", [(0, 1), (1, 0)])
    groups = exchange_groups()
    sent = pl.pallas_call(
        lookup_kernel,
        out_shape=jax.ShapeDtypeStruct((MEMBERS, 16, PART), f32),
        in_specs=[SCALARS] + [FULL] * 3,
        out_specs=FULL,
        compiler_params=PARAMS,
        name="lookup",
    )(where, active_slots.reshape(8, 128), table, other)
    received = lax.all_to_all(sent, AXES, 0, 0, axis_index_groups=groups)
    partial = pl.pallas_call(
        force_kernel,
        out_shape=jax.ShapeDtypeStruct((MEMBERS, 16, PART), f32),
        in_specs=[FULL] * 3,
        out_specs=FULL,
        scratch_shapes=[
            pltpu.VMEM((80, SOURCES), bf16),
            pltpu.VMEM((32, SOURCES), bf16),
            pltpu.VMEM((32, SOURCES), bf16),
            pltpu.VMEM((32, PART), f32),
        ],
        compiler_params=PARAMS,
        name="forces",
    )(received, table, other)
    shares = lax.all_to_all(partial, AXES, 0, 0, axis_index_groups=groups)
    half_result = pl.pallas_call(
        correct_kernel,
        out_shape=jax.ShapeDtypeStruct((12, HALF), f32),
        in_specs=[FULL],
        out_specs=FULL,
        compiler_params=PARAMS,
        name="corrector",
    )(shares)
    halves = lax.all_gather(half_result, "core")
    result = jnp.concatenate([halves[0], halves[1]], 1)
    return jnp.where((active_slots >= 0)[None, :], result, 0.0)


def solution(mesh):
    split_mesh = Mesh(mesh.devices.reshape(SIZES), AXES)
    return jax.shard_map(
        local,
        mesh=split_mesh,
        in_specs=(P(None, BLK), P(BLK), P(BLK), P(ACT)),
        out_specs=P(None, ACT),
        check_vma=False,
    )
```

time: 383 us -> 101 us (0.26)
  the two profiles are of different devices: /device:TPU:417 before, /device:TPU:33 now
where the time goes in v1:
time: 101 us; the launch traced here: 100 us
  blocking collectives  44.5 us (44%)
  waiting for transfers between devices  22.8 us (23%)
  Pallas kernels  22.4 us (22%)
  starting transfers between devices  7 us (7%)
  local copies, waits for them, and re-layouts  2.57 us (3%)
    all_to_all x1, blocking collectives, local(): received = lax.all_to_all(sent, AXES, 0, 0, axis_index_groups=groups)  42.4 us
    all_to_all x1, waiting for transfers between devices, local(): shares = lax.all_to_all(partial, AXES, 0, 0, axis_index_groups=groups)  21.4 us
    pallas_call x1, Pallas kernels, local(): pl.pallas_call(force_kernel, out_shape=jax.ShapeDtypeStruct((MEMBERS, 16,...  16.6 us
    pallas_call x1, Pallas kernels, local(): pl.pallas_call(lookup_kernel, out_shape=jax.ShapeDtypeStruct((MEMBERS, 16...  5.09 us
    all_to_all x1, starting transfers between devices, local(): shares = lax.all_to_all(partial, AXES, 0, 0, axis_index_groups=groups)  4.42 us
    ppermute x1, starting transfers between devices, local(): other = lax.ppermute(table, 'core', [(0, 1), (1, 0)])  2.58 us
    unnamed x8, local copies, waits for them, and re-layouts  2.56 us
    all_gather x1, blocking collectives, local(): halves = lax.all_gather(half_result, 'core')  2.09 us
  transfers between devices with their start and end apart: 2, of which 2 were waited for; matrix products, arithmetic and copies ran while one was open for 0% of the time, Pallas kernels for 0%

profile of v1, /device:TPU:33, one launch (start us, length us, event | category | flops | bytes accessed | tf_op | source)
XLA Modules:
  0.0 100.1 jit_solution(16833683946789165381)
XLA Ops:
  0.0 0.0 copy-start
  0.0 1.0 %copy-done = f32[12,8192]{1,0:T(8,128)S(1)} copy-done((f32[12,8192]{1,0:T(8,128)S(1)}, f32[12,8192]{1,0:T(8,128)}, u32[]{:S(2)}) %copy-start) | copy-done | bytes 393240
  1.0 0.0 copy-start.1
  1.0 0.8 copy-done.1
  1.8 0.0 copy-start.2
  1.8 0.8 copy-done.2
  2.6 0.6 table.1.mine
  3.2 2.6 %collective-permute-start = (f32[16,8192]{1,0:T(8,128)S(1)}, f32[16,8192]{1,0:T(8,128)S(1)}, u32[]{:S(2)}, u32[]{:S(2)}) collective-permute-start(f32[16,8192]{1,0:T(8,128)S(1)} %table.1.mine), channel_id=1, source_target_pairs={{0,32},{32,0},{1,33},{33,1},{2,34},{34,2},{3,35},{35,3},{4,36},{36... | collective-permute-start | bytes 1572872 | tf_op jit(solution)/shard_map/ppermute | solution.py:243
  5.8 0.0 copy-start.3
  5.8 0.1 pad_add_fusion.where
  5.9 1.4 %collective-permute-done.other = f32[16,8192]{1,0:T(8,128)S(1)} collective-permute-done((f32[16,8192]{1,0:T(8,128)S(1)}, f32[16,8192]{1,0:T(8,128)S(1)}, u32[]{:S(2)}, u32[]{:S(2)}) %collective-permute-start) | collective-permute-done | bytes 524320 | tf_op jit(solution)/shard_map/ppermute | solution.py:243
  7.3 0.0 copy-done.3
  7.3 5.1 %lookup.1 = f32[16,16,256]{2,1,0:T(8,128)S(1)} custom-call(s32[2]{0:T(128)S(1)} %pad_add_fusion.where, s32[8,128]{1,0:T(8,128)S(1)} %bitcast.13, f32[16,8192]{1,0:T(8,128)S(1)} %table.1.mine, f32[16,8192]{1,0:T(8,128)S(1)} %collective-permute-done.other), custom_call_target="tpu_custom_call" | custom-call | tf_op jit(solution)/shard_map/lookup/pallas_call | solution.py:245
  12.4 42.4 %all_to_all.10.received = f32[16,16,256]{2,1,0:T(8,128)S(1)} all-to-all(f32[16,16,256]{2,1,0:T(8,128)S(1)} %lookup.1), channel_id=1, replica_groups={{0,24,64,88,128,152,192,216,256,280,320,344,384,408,448,472},{1,25,65,8..., dimensions={0} | all-to-all | bytes 524288 | tf_op jit(solution)/shard_map/all_to_all | solution.py:253
  54.8 16.6 %forces.1 = f32[16,16,256]{2,1,0:T(8,128)} custom-call(f32[16,16,256]{2,1,0:T(8,128)S(1)} %all_to_all.10.received, f32[16,8192]{1,0:T(8,128)S(1)} %table.1.mine, f32[16,8192]{1,0:T(8,128)S(1)} %collective-permute-done.other), custom_call_target="tpu_custom_call" | custom-call | tf_op jit(solution)/shard_map/forces/pallas_call | solution.py:254
  71.4 4.4 %all-to-all-start.1 = ((f32[16,16,256]{2,1,0:T(8,128)}), f32[16,16,256]{2,1,0:T(8,128)S(1)}, u32[]{:S(2)}, u32[]{:S(2)}) async-start(f32[16,16,256]{2,1,0:T(8,128)} %forces.1), calls=%async_computation.1 | async-start | bytes 524288 | tf_op jit(solution)/shard_map/all_to_all | solution.py:268
  75.9 21.4 %all-to-all-done.1.received = f32[16,16,256]{2,1,0:T(8,128)S(1)} async-done(((f32[16,16,256]{2,1,0:T(8,128)}), f32[16,16,256]{2,1,0:T(8,128)S(1)}, u32[]{:S(2)}, u32[]{:S(2)}) %all-to-all-start.1) | async-done | bytes 262176 | tf_op jit(solution)/shard_map/all_to_all | solution.py:268
  97.3 2.1 %all-gather.1 = f32[2,12,512]{2,1,0:T(8,128)S(1)} all-gather(f32[1,12,512]{2,1,0:T(8,128)S(1)} %bitcast.10), channel_id=2, replica_groups=mesh['y'=4,'zh'=2,'core'=2,'xh'=2,'xl'=2,'zl'=8] {'core'}, dimensions={0}, use_global_device_ids=true | all-gather | bytes 73728 | tf_op jit(solution)/shard_map/all_gather | solution.py:277
  99.4 0.6 maximum_select_fusion
  (3 shorter events, 0.0 us)
Async XLA Ops:
  0.0 1.0 %copy-start = (f32[12,8192]{1,0:T(8,128)S(1)}, f32[12,8192]{1,0:T(8,128)}, u32[]{:S(2)}) copy-start(f32[12,8192]{1,0:T(8,128)} %state.1) | copy-start | bytes 1179652
  1.0 0.8 copy-start.1
  1.8 0.8 copy-start.2
  3.2 4.1 %collective-permute-start = (f32[16,8192]{1,0:T(8,128)S(1)}, f32[16,8192]{1,0:T(8,128)S(1)}, u32[]{:S(2)}, u32[]{:S(2)}) collective-permute-start(f32[16,8192]{1,0:T(8,128)S(1)} %table.1.mine), channel_id=1, source_target_pairs={{0,32},{32,0},{1,33},{33,1},{2,34},{34,2},{3,35},{35,3},{4,36},{36... | collective-permute-start | bytes 1572872 | tf_op jit(solution)/shard_map/ppermute | solution.py:243
  5.8 1.5 %copy-start.3 = (s32[1024]{0:T(1024)S(1)}, s32[1024]{0:T(1024)}, u32[]{:S(2)}) copy-start(s32[1024]{0:T(1024)} %param.7) | copy-start | bytes 12292
  71.4 25.9 %all-to-all-start.1 = ((f32[16,16,256]{2,1,0:T(8,128)}), f32[16,16,256]{2,1,0:T(8,128)S(1)}, u32[]{:S(2)}, u32[]{:S(2)}) async-start(f32[16,16,256]{2,1,0:T(8,128)} %forces.1), calls=%async_computation.1 | async-start | bytes 524288 | tf_op jit(solution)/shard_map/all_to_all | solution.py:268

commit v2 on v1

--- a/solution.py
+++ b/solution.py
@@ -20,6 +20,7 @@
 SHARD = 8192
 HALF = 512
 PART = 256
+SENDERS = 8
 MEMBERS = 16
 CHUNK = 512
 SOURCES = 2 * SHARD
@@ -63,7 +64,17 @@
     return high, (value - high.astype(f32)).astype(bf16)
 
 
-def table_kernel(state, mass, level, table):
+def table_kernel(state_in, mass_in, level_in, table, state, mass, level, done):
+    copies = [
+        pltpu.make_async_copy(source, target, done.at[k])
+        for k, (source, target) in enumerate(
+            ((state_in, state), (mass_in, mass), (level_in, level))
+        )
+    ]
+    for copy in copies:
+        copy.start()
+    for copy in copies:
+        copy.wait()
     lev = level[...]
     dt = jnp.where(lev == 0, 0.375, jnp.where(lev == 3, 0.0625, 0.125)).astype(f32)
     x, v, a, j = state[0:3], state[3:6], state[6:9], state[9:12]
@@ -81,43 +92,29 @@
     table[15:16, :] = 3.0 * jnp.sum(place * speed, 0, keepdims=True)
 
 
-def lookup_kernel(where, slots, mine, other, out):
-    first, core = where[0], where[1]
-    tables = ((mine, first + core * SHARD), (other, first + (1 - core) * SHARD))
-    groups = HALF // 128
-    index = slots[pl.ds(core * groups, groups), :]
-    picked = [(jnp.zeros((8, 128), f32),) * 2 for _ in range(groups)]
-    for table, start in tables:
+def lookup_kernel(where, own_slots, passed_slots, mine, other, out):
+    first, core, helper = where[0], where[1], where[2]
+    at = pl.ds(core * 4 + helper * 2, 2)
+    index = jnp.where(helper == 0, own_slots[at, :], passed_slots[at, :])
+    index = jnp.concatenate((index[0:1], index[1:2]), 1)
+    picked = jnp.zeros((16, PART), f32)
+    for table, start in ((mine, first + core * SHARD), (other, first + (1 - core) * SHARD)):
         local_index = index - start
-        low = [jnp.broadcast_to((local_index & 127)[g : g + 1], (8, 128)) for g in range(groups)]
-        high = [jnp.broadcast_to((local_index >> 7)[g : g + 1], (8, 128)) for g in range(groups)]
-
-        def look(h, carry):
-            at = pl.ds(pl.multiple_of(h * 128, 128), 128)
-            tiles = (table[0:8, at], table[8:16, at])
-            result = []
-            for g in range(groups):
-                hit = high[g] == h
-                result.append(
-                    tuple(
-                        jnp.where(
-                            hit,
-                            jnp.take_along_axis(
-                                tiles[k], low[g], axis=1, mode="promise_in_bounds"
-                            ),
-                            carry[g][k],
-                        )
-                        for k in range(2)
-                    )
-                )
-            return result
-
-        picked = lax.fori_loop(0, SHARD // 128, look, picked, unroll=4)
-    for member in range(MEMBERS):
-        for part in range(2):
-            g = (member % 2) * 2 + part
-            for k in range(2):
-                out[member, 8 * k : 8 * k + 8, part * 128 : (part + 1) * 128] = picked[g][k]
+        low, high = local_index & 127, local_index >> 7
+        low = jnp.broadcast_to(low, (128, PART))
+        hit = jnp.where(rows_of(low) == low, 1.0, 0.0).astype(bf16)
+        hits = jnp.concatenate((hit, hit, hit), 0)
+        high = jnp.broadcast_to(high, (16, PART))
+        for block in range(SHARD // 2048):
+            tiles = [
+                table[:, (block * 16 + i) * 128 : (block * 16 + i + 1) * 128] for i in range(16)
+            ]
+            parts = [part.astype(bf16) for part in split(jnp.concatenate(tiles, 0))]
+            found = dot(jnp.concatenate(parts, 1), hits, NN)
+            for i in range(16):
+                picked = jnp.where(high == block * 16 + i, found[16 * i : 16 * i + 16], picked)
+    for member in range(SENDERS):
+        out[member] = picked
 
 
 def source_features(table, features, pull, swing, offset):
@@ -169,11 +166,12 @@
     return result
 
 
-def force_kernel(received, mine, other, out, features, pull, swing, total):
+def force_kernel(where, received, mine, other, out, features, pull, swing, total, rows):
     target_rows = received[0]
-    for sender in range(2, MEMBERS, 2):
+    for sender in range(1, SENDERS):
         target_rows = target_rows + received[sender]
     target = target_rows[0:8]
+    rows[...] = target_rows
     source_features(mine, features, pull, swing, 0)
     source_features(other, features, pull, swing, SHARD)
     radius_part, near_part = target_features(target)
@@ -201,26 +199,26 @@
     place, speed = target[0:3], target[3:6]
     accel = sums[0:3] - place * sums[6:7]
     jerk = sums[3:6] - speed * sums[6:7] + place * sums[7:8]
+    spare = rows[pl.ds(7 + where[3], 1), :]
     for member in range(MEMBERS):
         out[member, 0:3, :] = accel
         out[member, 3:6, :] = jerk
-        out[member, 6:8, :] = target[6:8]
-        out[member, 8:16, :] = target_rows[8:16]
+        out[member, 6:7, :] = spare
+        out[member, 7:8, :] = spare
 
 
 def correct_kernel(received, out):
     for part in range(2):
-        rows = received[part]
-        force = rows[0:8]
-        for sender in range(part + 2, MEMBERS, 2):
-            force = force + received[sender, 0:8, :]
-        dt = rows[7:8]
+        force = received[part]
+        for sender in range(1, SENDERS):
+            force = force + received[2 * sender + part]
+        dt = received[part, 6:7, :]
+        bases = [received[2 * sender + part, 6:7, :] for sender in range(1, 7)]
         accel, jerk = force[0:3], force[3:6]
         half = 0.5 * dt
         step_sq = dt * dt * ONE_TWELFTH
-        velocity = rows[11:14] + half * accel - step_sq * jerk
-        base = rows[8:11]
-        position = base + half * velocity - step_sq * accel
+        velocity = jnp.concatenate(bases[3:6], 0) + half * accel - step_sq * jerk
+        position = jnp.concatenate(bases[0:3], 0) + half * velocity - step_sq * accel
         at = slice(part * PART, (part + 1) * PART)
         out[0:3, at] = position
         out[3:6, at] = velocity
@@ -229,43 +227,52 @@
 
 
 def local(star_state, star_mass, star_level, active_slots):
-    core = lax.axis_index("core")
-    pair = lax.axis_index("y") * 2 + lax.axis_index("zh")
-    where = jnp.stack([pair * SOURCES, core]).astype(jnp.int32)
+    core, helper = lax.axis_index("core"), lax.axis_index("xh")
+    sender = lax.axis_index("y") * 2 + lax.axis_index("zh")
+    where = jnp.stack([sender * SOURCES, core, helper, sender]).astype(jnp.int32)
+    slots = active_slots.reshape(8, 128)
+    passed = lax.ppermute(slots, ("xh", "xl"), [(x, 3 - x) for x in range(4)])
+    anywhere = pl.BlockSpec(memory_space=pl.ANY)
     table = pl.pallas_call(
         table_kernel,
         out_shape=jax.ShapeDtypeStruct((16, SHARD), f32),
-        in_specs=[FULL] * 3,
-        out_specs=FULL,
+        in_specs=[anywhere] * 3,
+        out_specs=FULL,
+        scratch_shapes=[
+            pltpu.VMEM((12, SHARD), f32),
+            pltpu.VMEM((1, SHARD), f32),
+            pltpu.VMEM((1, SHARD), jnp.int32),
+            pltpu.SemaphoreType.DMA((3,)),
+        ],
         compiler_params=PARAMS,
         name="table",
     )(star_state, star_mass.reshape(1, SHARD), star_level.reshape(1, SHARD))
     other = lax.ppermute(table, "core", [(0, 1), (1, 0)])
-    groups = exchange_groups()
     sent = pl.pallas_call(
         lookup_kernel,
-        out_shape=jax.ShapeDtypeStruct((MEMBERS, 16, PART), f32),
-        in_specs=[SCALARS] + [FULL] * 3,
+        out_shape=jax.ShapeDtypeStruct((SENDERS, 16, PART), f32),
+        in_specs=[SCALARS] + [FULL] * 4,
         out_specs=FULL,
         compiler_params=PARAMS,
         name="lookup",
-    )(where, active_slots.reshape(8, 128), table, other)
-    received = lax.all_to_all(sent, AXES, 0, 0, axis_index_groups=groups)
+    )(where, slots, passed, table, other)
+    received = lax.all_to_all(sent, ("y", "zh"), 0, 0)
     partial = pl.pallas_call(
         force_kernel,
-        out_shape=jax.ShapeDtypeStruct((MEMBERS, 16, PART), f32),
-        in_specs=[FULL] * 3,
+        out_shape=jax.ShapeDtypeStruct((MEMBERS, 8, PART), f32),
+        in_specs=[SCALARS] + [FULL] * 3,
         out_specs=FULL,
         scratch_shapes=[
             pltpu.VMEM((80, SOURCES), bf16),
             pltpu.VMEM((32, SOURCES), bf16),
             pltpu.VMEM((32, SOURCES), bf16),
             pltpu.VMEM((32, PART), f32),
+            pltpu.VMEM((16, PART), f32),
         ],
         compiler_params=PARAMS,
         name="forces",
-    )(received, table, other)
-    shares = lax.all_to_all(partial, AXES, 0, 0, axis_index_groups=groups)
+    )(where, received, table, other)
+    shares = lax.all_to_all(partial, AXES, 0, 0, axis_index_groups=exchange_groups())
     half_result = pl.pallas_call(
         correct_kernel,
         out_shape=jax.ShapeDtypeStruct((12, HALF), f32),

time: 101 us -> 92.2 us (0.913)
  waiting for transfers between devices: 22.8 us -> 17.3 us
  starting transfers between devices: 7 us -> 11.8 us
  blocking collectives: 44.5 us -> 40 us
  Pallas kernels: 22.4 us -> 19.3 us
    all_to_all x1, blocking collectives: 42.4 us -> 30.6 us  [local(): received = lax.all_to_all(sent, ('y', 'zh'), 0, 0)]
    all_gather x1, blocking collectives: 2.09 us -> 9.45 us  [local(): halves = lax.all_gather(half_result, 'core')]
    all_to_all x1, waiting for transfers between devices: 21.4 us -> 16.2 us  [local(): lax.all_to_all(partial, AXES, 0, 0, axis_index_groups=exchange_groups())]
    ppermute x0 -> x1, starting transfers between devices: none -> 4.39 us  [local(): passed = lax.ppermute(slots, ('xh', 'xl'), [(x, 3 - x) for x in range(4)])]
    pallas_call x2, Pallas kernels: 21.7 us -> 18.5 us  [the longest x1 17.2 us: local(): pl.pallas_call(force_kernel, out_shape=jax.ShapeDtypeStruct((MEMBERS, 8,...]
    ppermute x1, waiting for transfers between devices: 1.42 us -> 0.01 us  [local(): other = lax.ppermute(table, 'core', [(0, 1), (1, 0)])]
    ppermute x0 -> x1, waiting for transfers between devices: none -> 1.08 us  [local(): passed = lax.ppermute(slots, ('xh', 'xl'), [(x, 3 - x) for x in range(4)])]
  transfers between devices with their start and end apart: 2 -> 3, of which waited for: 2 -> 2; matrix products, arithmetic and copies ran while one was open for 0% -> 0% of each run, Pallas kernels for 0% -> 0%
where the time goes in v2:
time: 92.2 us; the launch traced here: 91.8 us
  blocking collectives  40 us (43%)
  Pallas kernels  19.3 us (21%)
  waiting for transfers between devices  17.3 us (19%)
  starting transfers between devices  11.8 us (13%)
  local copies, waits for them, and re-layouts  2.56 us (3%)
    all_to_all x1, blocking collectives, local(): received = lax.all_to_all(sent, ('y', 'zh'), 0, 0)  30.6 us
    pallas_call x1, Pallas kernels, local(): pl.pallas_call(force_kernel, out_shape=jax.ShapeDtypeStruct((MEMBERS, 8,...  17.2 us
    all_to_all x1, waiting for transfers between devices, local(): lax.all_to_all(partial, AXES, 0, 0, axis_index_groups=exchange_groups())  16.2 us
    all_gather x1, blocking collectives, local(): halves = lax.all_gather(half_result, 'core')  9.45 us
    all_to_all x1, starting transfers between devices, local(): lax.all_to_all(partial, AXES, 0, 0, axis_index_groups=exchange_groups())  4.85 us
    ppermute x1, starting transfers between devices, local(): passed = lax.ppermute(slots, ('xh', 'xl'), [(x, 3 - x) for x in range(4)])  4.39 us
    ppermute x1, starting transfers between devices, local(): other = lax.ppermute(table, 'core', [(0, 1), (1, 0)])  2.58 us
    unnamed x8, local copies, waits for them, and re-layouts  2.56 us
  transfers between devices with their start and end apart: 3, of which 2 were waited for; matrix products, arithmetic and copies ran while one was open for 0% of the time, Pallas kernels for 0%

profile of v2, /device:TPU:33, one launch (start us, length us, event | category | flops | bytes accessed | tf_op | source)
XLA Modules:
  0.0 91.8 jit_solution(5220707003329170828)
XLA Ops:
  0.0 0.0 copy-start
  0.0 1.0 %copy-done = f32[12,8192]{1,0:T(8,128)S(1)} copy-done((f32[12,8192]{1,0:T(8,128)S(1)}, f32[12,8192]{1,0:T(8,128)}, u32[]{:S(2)}) %copy-start) | copy-done | bytes 393240
  1.0 0.0 copy-start.1
  1.0 0.8 copy-done.1
  1.8 0.0 copy-start.2
  1.8 0.8 copy-done.2
  2.6 0.0 copy-start.3
  2.6 0.8 table.1.mine
  3.3 2.6 %collective-permute-start.1 = (f32[16,8192]{1,0:T(8,128)S(1)}, f32[16,8192]{1,0:T(8,128)S(1)}, u32[]{:S(2)}, u32[]{:S(2)}) collective-permute-start(f32[16,8192]{1,0:T(8,128)S(1)} %table.1.mine), channel_id=1, source_target_pairs={{0,32},{32,0},{1,33},{33,1},{2,34},{34,2},{3,35},{35,3},{4,36},{36... | collective-permute-start | bytes 1572872 | tf_op jit(solution)/shard_map/ppermute | solution.py:250
  5.9 0.0 copy-done.3
  5.9 4.4 %collective-permute-start = (s32[8,128]{1,0:T(8,128)S(1)}, s32[8,128]{1,0:T(8,128)S(1)}, u32[]{:S(2)}, u32[]{:S(2)}) collective-permute-start(s32[8,128]{1,0:T(8,128)S(1)} %bitcast.15), channel_id=1, source_target_pairs={{0,24},{8,16},{16,8},{24,0},{1,25},{9,17},{17,9},{25,1},{2,26},{10... | collective-permute-start | bytes 12296 | tf_op jit(solution)/shard_map/ppermute | solution.py:234
  10.4 0.1 pad_add_fusion.where
  10.4 1.1 %collective-permute-done.passed_slots = s32[8,128]{1,0:T(8,128)S(1)} collective-permute-done((s32[8,128]{1,0:T(8,128)S(1)}, s32[8,128]{1,0:T(8,128)S(1)}, u32[]{:S(2)}, u32[]{:S(2)}) %collective-permute-start) | collective-permute-done | bytes 4128 | tf_op jit(solution)/shard_map/ppermute | solution.py:234
  11.5 0.0 collective-permute-done.1.other
  11.5 1.3 %lookup.1 = f32[8,16,256]{2,1,0:T(8,128)S(1)} custom-call(s32[4]{0:T(128)S(1)} %pad_add_fusion.where, s32[8,128]{1,0:T(8,128)S(1)} %bitcast.16, s32[8,128]{1,0:T(8,128)S(1)} %collective-permute-done.passed_slots, f32[16,8192]{1,0:T(8,128)S(1)} %table.1.mine, f32[16,8192]{1,0:T(8,128)S(1)} %collective-permute-done.1.other), custom_call_target="tpu_custom_call" | custom-call | tf_op jit(solution)/shard_map/lookup/pallas_call | solution.py:251
  12.8 30.6 %all_to_all.10.received = f32[8,16,256]{2,1,0:T(8,128)S(1)} all-to-all(f32[8,16,256]{2,1,0:T(8,128)S(1)} %lookup.1), channel_id=1, replica_groups=mesh['y'=4,'zh'=2,'core'=2,'xh'=2,'xl'=2,'zl'=8] {'y','zh'}, dimensions={0} | all-to-all | bytes 262144 | tf_op jit(solution)/shard_map/all_to_all | solution.py:259
  43.4 17.2 %forces.1 = f32[16,8,256]{2,1,0:T(8,128)} custom-call(s32[4]{0:T(128)S(1)} %pad_add_fusion.where, f32[8,16,256]{2,1,0:T(8,128)S(1)} %all_to_all.10.received, f32[16,8192]{1,0:T(8,128)S(1)} %table.1.mine, f32[16,8192]{1,0:T(8,128)S(1)} %collective-permute-done.1.other), custom_call_target="tpu_custom_call" | custom-call | tf_op jit(solution)/shard_map/forces/pallas_call | solution.py:260
  60.6 4.8 %all-to-all-start.1 = ((f32[16,8,256]{2,1,0:T(8,128)}), f32[16,8,256]{2,1,0:T(8,128)S(1)}, u32[]{:S(2)}, u32[]{:S(2)}) async-start(f32[16,8,256]{2,1,0:T(8,128)} %forces.1), calls=%async_computation.1 | async-start | bytes 262144 | tf_op jit(solution)/shard_map/all_to_all | solution.py:275
  65.5 16.2 %all-to-all-done.1.received = f32[16,8,256]{2,1,0:T(8,128)S(1)} async-done(((f32[16,8,256]{2,1,0:T(8,128)}), f32[16,8,256]{2,1,0:T(8,128)S(1)}, u32[]{:S(2)}, u32[]{:S(2)}) %all-to-all-start.1) | async-done | bytes 131104 | tf_op jit(solution)/shard_map/all_to_all | solution.py:275
  81.7 9.5 %all-gather.1 = f32[2,12,512]{2,1,0:T(8,128)S(1)} all-gather(f32[1,12,512]{2,1,0:T(8,128)S(1)} %bitcast.12), channel_id=2, replica_groups=mesh['y'=4,'zh'=2,'core'=2,'xh'=2,'xl'=2,'zl'=8] {'core'}, dimensions={0}, use_global_device_ids=true | all-gather | bytes 73728 | tf_op jit(solution)/shard_map/all_gather | solution.py:284
  91.1 0.6 maximum_select_fusion
  (3 shorter events, 0.0 us)
Async XLA Ops:
  0.0 1.0 %copy-start = (f32[12,8192]{1,0:T(8,128)S(1)}, f32[12,8192]{1,0:T(8,128)}, u32[]{:S(2)}) copy-start(f32[12,8192]{1,0:T(8,128)} %state_in.1) | copy-start | bytes 1179652
  1.0 0.8 copy-start.1
  1.8 0.8 copy-start.2
  2.6 3.4 %copy-start.3 = (s32[1024]{0:T(1024)S(1)}, s32[1024]{0:T(1024)}, u32[]{:S(2)}) copy-start(s32[1024]{0:T(1024)} %param.7) | copy-start | bytes 12292
  3.3 8.2 %collective-permute-start.1 = (f32[16,8192]{1,0:T(8,128)S(1)}, f32[16,8192]{1,0:T(8,128)S(1)}, u32[]{:S(2)}, u32[]{:S(2)}) collective-permute-start(f32[16,8192]{1,0:T(8,128)S(1)} %table.1.mine), channel_id=1, source_target_pairs={{0,32},{32,0},{1,33},{33,1},{2,34},{34,2},{3,35},{35,3},{4,36},{36... | collective-permute-start | bytes 1572872 | tf_op jit(solution)/shard_map/ppermute | solution.py:250
  5.9 5.6 %collective-permute-start = (s32[8,128]{1,0:T(8,128)S(1)}, s32[8,128]{1,0:T(8,128)S(1)}, u32[]{:S(2)}, u32[]{:S(2)}) collective-permute-start(s32[8,128]{1,0:T(8,128)S(1)} %bitcast.15), channel_id=1, source_target_pairs={{0,24},{8,16},{16,8},{24,0},{1,25},{9,17},{17,9},{25,1},{2,26},{10... | collective-permute-start | bytes 12296 | tf_op jit(solution)/shard_map/ppermute | solution.py:234
  60.6 21.0 %all-to-all-start.1 = ((f32[16,8,256]{2,1,0:T(8,128)}), f32[16,8,256]{2,1,0:T(8,128)S(1)}, u32[]{:S(2)}, u32[]{:S(2)}) async-start(f32[16,8,256]{2,1,0:T(8,128)} %forces.1), calls=%async_computation.1 | async-start | bytes 262144 | tf_op jit(solution)/shard_map/all_to_all | solution.py:275

commit v3 on v2

--- a/solution.py
+++ b/solution.py
@@ -194,7 +194,7 @@
         )
         return 0
 
-    lax.fori_loop(0, SOURCES // CHUNK, step, 0, unroll=2)
+    lax.fori_loop(0, SOURCES // CHUNK, step, 0, unroll=16)
     sums = total[0:8] + total[8:16] + total[16:24]
     place, speed = target[0:3], target[3:6]
     accel = sums[0:3] - place * sums[6:7]
@@ -245,8 +245,12 @@
             pltpu.SemaphoreType.DMA((3,)),
         ],
         compiler_params=PARAMS,
+        cost_estimate=pl.CostEstimate(
+            flops=10**10, bytes_accessed=120 * SHARD, transcendentals=0
+        ),
         name="table",
     )(star_state, star_mass.reshape(1, SHARD), star_level.reshape(1, SHARD))
+    table, passed = lax.optimization_barrier((table, passed))
     other = lax.ppermute(table, "core", [(0, 1), (1, 0)])
     sent = pl.pallas_call(
         lookup_kernel,

time: 92.2 us -> 86.8 us (0.941)
  Pallas kernels: 19.3 us -> 14.3 us
  starting transfers between devices: 11.8 us -> 10.8 us
    pallas_call x1, Pallas kernels: 17.2 us -> 12.2 us  [local(): pl.pallas_call(force_kernel, out_shape=jax.ShapeDtypeStruct((MEMBERS, 8,...]
    ppermute x1, waiting for transfers between devices: 0.01 us -> 1.42 us  [local(): other = lax.ppermute(table, 'core', [(0, 1), (1, 0)])]
    all_to_all x1, starting transfers between devices: 4.85 us -> 3.55 us  [local(): lax.all_to_all(partial, AXES, 0, 0, axis_index_groups=exchange_groups())]
    ppermute x1, waiting for transfers between devices: 1.08 us -> 0.01 us  [local(): passed = lax.ppermute(slots, ('xh', 'xl'), [(x, 3 - x) for x in range(4)])]
  transfers between devices with their start and end apart: 3 -> 3, of which waited for: 2 -> 2; matrix products, arithmetic and copies ran while one was open for 0% -> 0% of each run, Pallas kernels for 0% -> 1%
where the time goes in v3:
time: 86.8 us; the launch traced here: 86.3 us
  blocking collectives  40.3 us (46%)
  waiting for transfers between devices  17.6 us (20%)
  Pallas kernels  14.3 us (16%)
  starting transfers between devices  10.8 us (12%)
  local copies, waits for them, and re-layouts  2.56 us (3%)
    all_to_all x1, blocking collectives, local(): received = lax.all_to_all(sent, ('y', 'zh'), 0, 0)  30.6 us
    all_to_all x1, waiting for transfers between devices, local(): lax.all_to_all(partial, AXES, 0, 0, axis_index_groups=exchange_groups())  16.2 us
    pallas_call x1, Pallas kernels, local(): pl.pallas_call(force_kernel, out_shape=jax.ShapeDtypeStruct((MEMBERS, 8,...  12.2 us
    all_gather x1, blocking collectives, local(): halves = lax.all_gather(half_result, 'core')  9.65 us
    ppermute x1, starting transfers between devices, local(): passed = lax.ppermute(slots, ('xh', 'xl'), [(x, 3 - x) for x in range(4)])  4.38 us
    all_to_all x1, starting transfers between devices, local(): lax.all_to_all(partial, AXES, 0, 0, axis_index_groups=exchange_groups())  3.55 us
    ppermute x1, starting transfers between devices, local(): other = lax.ppermute(table, 'core', [(0, 1), (1, 0)])  2.86 us
    unnamed x8, local copies, waits for them, and re-layouts  2.56 us
  transfers between devices with their start and end apart: 3, of which 2 were waited for; matrix products, arithmetic and copies ran while one was open for 0% of the time, Pallas kernels for 1%

profile of v3, /device:TPU:33, one launch (start us, length us, event | category | flops | bytes accessed | tf_op | source)
XLA Modules:
  0.0 86.3 jit_solution(750282746416556340)
XLA Ops:
  0.0 4.4 %collective-permute-start = (s32[8,128]{1,0:T(8,128)}, s32[8,128]{1,0:T(8,128)S(1)}, u32[]{:S(2)}, u32[]{:S(2)}) collective-permute-start(s32[8,128]{1,0:T(8,128)} %bitcast.13), channel_id=1, source_target_pairs={{0,24},{8,16},{16,8},{24,0},{1,25},{9,17},{17,9},{25,1},{2,26},{10... | collective-permute-start | bytes 12296 | tf_op jit(solution)/shard_map/ppermute | solution.py:234
  4.4 0.0 copy-start.1
  4.4 1.0 %copy-done.1 = f32[12,8192]{1,0:T(8,128)S(1)} copy-done((f32[12,8192]{1,0:T(8,128)S(1)}, f32[12,8192]{1,0:T(8,128)}, u32[]{:S(2)}) %copy-start.1) | copy-done | bytes 393240
  5.4 0.0 copy-start.2
  5.4 0.8 copy-done.2
  6.2 0.0 copy-start.3
  6.2 0.8 copy-done.3
  6.9 0.8 table.1.mine
  7.7 0.0 collective-permute-done.passed_slots
  7.7 2.9 %collective-permute-start.1 = (f32[16,8192]{1,0:T(8,128)S(1)}, f32[16,8192]{1,0:T(8,128)S(1)}, u32[]{:S(2)}, u32[]{:S(2)}) collective-permute-start(f32[16,8192]{1,0:T(8,128)S(1)} %table.1.mine), channel_id=1, source_target_pairs={{0,32},{32,0},{1,33},{33,1},{2,34},{34,2},{3,35},{35,3},{4,36},{36... | collective-permute-start | bytes 1572872 | tf_op jit(solution)/shard_map/ppermute | solution.py:254
  10.6 0.0 copy-start
  10.6 0.1 pad_add_fusion.where
  10.7 1.4 %collective-permute-done.1.other = f32[16,8192]{1,0:T(8,128)S(1)} collective-permute-done((f32[16,8192]{1,0:T(8,128)S(1)}, f32[16,8192]{1,0:T(8,128)S(1)}, u32[]{:S(2)}, u32[]{:S(2)}) %collective-permute-start.1) | collective-permute-done | bytes 524320 | tf_op jit(solution)/shard_map/ppermute | solution.py:254
  12.1 0.0 copy-done
  12.1 1.3 %lookup.1 = f32[8,16,256]{2,1,0:T(8,128)S(1)} custom-call(s32[4]{0:T(128)S(1)} %pad_add_fusion.where, s32[8,128]{1,0:T(8,128)S(1)} %bitcast.14, s32[8,128]{1,0:T(8,128)S(1)} %collective-permute-done.passed_slots, f32[16,8192]{1,0:T(8,128)S(1)} %table.1.mine, f32[16,8192]{1,0:T(8,128)S(1)} %collective-permute-done.1.other), custom_call_target="tpu_custom_call" | custom-call | tf_op jit(solution)/shard_map/lookup/pallas_call | solution.py:255
  13.5 30.6 %all_to_all.10.received = f32[8,16,256]{2,1,0:T(8,128)S(1)} all-to-all(f32[8,16,256]{2,1,0:T(8,128)S(1)} %lookup.1), channel_id=1, replica_groups=mesh['y'=4,'zh'=2,'core'=2,'xh'=2,'xl'=2,'zl'=8] {'y','zh'}, dimensions={0} | all-to-all | bytes 262144 | tf_op jit(solution)/shard_map/all_to_all | solution.py:263
  44.1 12.2 %forces.1 = f32[16,8,256]{2,1,0:T(8,128)} custom-call(s32[4]{0:T(128)S(1)} %pad_add_fusion.where, f32[8,16,256]{2,1,0:T(8,128)S(1)} %all_to_all.10.received, f32[16,8192]{1,0:T(8,128)S(1)} %table.1.mine, f32[16,8192]{1,0:T(8,128)S(1)} %collective-permute-done.1.other), custom_call_target="tpu_custom_call" | custom-call | tf_op jit(solution)/shard_map/forces/pallas_call | solution.py:264
  56.2 3.6 %all-to-all-start.1 = ((f32[16,8,256]{2,1,0:T(8,128)}), f32[16,8,256]{2,1,0:T(8,128)S(1)}, u32[]{:S(2)}, u32[]{:S(2)}) async-start(f32[16,8,256]{2,1,0:T(8,128)} %forces.1), calls=%async_computation.1 | async-start | bytes 262144 | tf_op jit(solution)/shard_map/all_to_all | solution.py:279
  59.8 16.2 %all-to-all-done.1.received = f32[16,8,256]{2,1,0:T(8,128)S(1)} async-done(((f32[16,8,256]{2,1,0:T(8,128)}), f32[16,8,256]{2,1,0:T(8,128)S(1)}, u32[]{:S(2)}, u32[]{:S(2)}) %all-to-all-start.1) | async-done | bytes 131104 | tf_op jit(solution)/shard_map/all_to_all | solution.py:279
  76.0 9.7 %all-gather.1 = f32[2,12,512]{2,1,0:T(8,128)S(1)} all-gather(f32[1,12,512]{2,1,0:T(8,128)S(1)} %bitcast.12), channel_id=2, replica_groups=mesh['y'=4,'zh'=2,'core'=2,'xh'=2,'xl'=2,'zl'=8] {'core'}, dimensions={0}, use_global_device_ids=true | all-gather | bytes 73728 | tf_op jit(solution)/shard_map/all_gather | solution.py:288
  85.7 0.6 maximum_select_fusion
  (3 shorter events, 0.0 us)
Async XLA Ops:
  0.0 7.7 %collective-permute-start = (s32[8,128]{1,0:T(8,128)}, s32[8,128]{1,0:T(8,128)S(1)}, u32[]{:S(2)}, u32[]{:S(2)}) collective-permute-start(s32[8,128]{1,0:T(8,128)} %bitcast.13), channel_id=1, source_target_pairs={{0,24},{8,16},{16,8},{24,0},{1,25},{9,17},{17,9},{25,1},{2,26},{10... | collective-permute-start | bytes 12296 | tf_op jit(solution)/shard_map/ppermute | solution.py:234
  4.4 1.0 %copy-start.1 = (f32[12,8192]{1,0:T(8,128)S(1)}, f32[12,8192]{1,0:T(8,128)}, u32[]{:S(2)}) copy-start(f32[12,8192]{1,0:T(8,128)} %state_in.1) | copy-start | bytes 1179652
  5.4 0.8 copy-start.2
  6.2 0.8 copy-start.3
  7.7 4.4 %collective-permute-start.1 = (f32[16,8192]{1,0:T(8,128)S(1)}, f32[16,8192]{1,0:T(8,128)S(1)}, u32[]{:S(2)}, u32[]{:S(2)}) collective-permute-start(f32[16,8192]{1,0:T(8,128)S(1)} %table.1.mine), channel_id=1, source_target_pairs={{0,32},{32,0},{1,33},{33,1},{2,34},{34,2},{3,35},{35,3},{4,36},{36... | collective-permute-start | bytes 1572872 | tf_op jit(solution)/shard_map/ppermute | solution.py:254
  10.6 1.5 %copy-start = (s32[1024]{0:T(1024)S(1)}, s32[1024]{0:T(1024)}, u32[]{:S(2)}) copy-start(s32[1024]{0:T(1024)} %param.7) | copy-start | bytes 12292
  56.2 19.7 %all-to-all-start.1 = ((f32[16,8,256]{2,1,0:T(8,128)}), f32[16,8,256]{2,1,0:T(8,128)S(1)}, u32[]{:S(2)}, u32[]{:S(2)}) async-start(f32[16,8,256]{2,1,0:T(8,128)} %forces.1), calls=%async_computation.1 | async-start | bytes 262144 | tf_op jit(solution)/shard_map/all_to_all | solution.py:279

commit v4 on v3

--- a/solution.py
+++ b/solution.py
@@ -22,6 +22,8 @@
 PART = 256
 SENDERS = 8
 MEMBERS = 16
+NEAR = 8
+Y_ORDER = (2, 1, 3, 0)
 CHUNK = 512
 SOURCES = 2 * SHARD
 FULL = pl.BlockSpec(memory_space=pltpu.VMEM)
@@ -32,20 +34,26 @@
 dot = functools.partial(lax.dot_general, preferred_element_type=f32)
 
 
-def exchange_groups():
+def exchange_groups(columns_of):
     groups = []
     for core in range(2):
-        for x in range(2):
+        for columns in columns_of:
             for zl in range(8):
                 groups.append(
                     [
                         (((y * 2 + zh) * 2 + core) * 4 + column) * 8 + zl
-                        for y in range(4)
-                        for zh in range(2)
-                        for column in (x, 3 - x)
+                        for zh in ((1, 0) if zl < NEAR else (0, 1))
+                        for y in Y_ORDER
+                        for column in columns
                     ]
                 )
     return groups
+
+
+def sender_of(y, zh, zl):
+    near = (zl < NEAR).astype(jnp.int32)
+    place = sum(jnp.where(y == value, k, 0) for k, value in enumerate(Y_ORDER))
+    return jnp.where(zh == near, 0, 4) + place
 
 
 def rows_of(value):
@@ -228,8 +236,9 @@
 
 def local(star_state, star_mass, star_level, active_slots):
     core, helper = lax.axis_index("core"), lax.axis_index("xh")
-    sender = lax.axis_index("y") * 2 + lax.axis_index("zh")
-    where = jnp.stack([sender * SOURCES, core, helper, sender]).astype(jnp.int32)
+    y, zh = lax.axis_index("y"), lax.axis_index("zh")
+    sender = sender_of(y, zh, lax.axis_index("zl"))
+    where = jnp.stack([(y * 2 + zh) * SOURCES, core, helper, sender]).astype(jnp.int32)
     slots = active_slots.reshape(8, 128)
     passed = lax.ppermute(slots, ("xh", "xl"), [(x, 3 - x) for x in range(4)])
     anywhere = pl.BlockSpec(memory_space=pl.ANY)
@@ -260,7 +269,8 @@
         compiler_params=PARAMS,
         name="lookup",
     )(where, slots, passed, table, other)
-    received = lax.all_to_all(sent, ("y", "zh"), 0, 0)
+    alone = exchange_groups([(x,) for x in range(4)])
+    received = lax.all_to_all(sent, AXES, 0, 0, axis_index_groups=alone)
     partial = pl.pallas_call(
         force_kernel,
         out_shape=jax.ShapeDtypeStruct((MEMBERS, 8, PART), f32),
@@ -276,7 +286,8 @@
         compiler_params=PARAMS,
         name="forces",
     )(where, received, table, other)
-    shares = lax.all_to_all(partial, AXES, 0, 0, axis_index_groups=exchange_groups())
+    paired = exchange_groups([(x, 3 - x) for x in range(2)])
+    shares = lax.all_to_all(partial, AXES, 0, 0, axis_index_groups=paired)
     half_result = pl.pallas_call(
         correct_kernel,
         out_shape=jax.ShapeDtypeStruct((12, HALF), f32),

time: 86.8 us -> 74.6 us (0.86)
  the two profiles are of different devices: /device:TPU:33 before, /device:TPU:449 now
where the time goes in v4:
time: 74.6 us; the launch traced here: 74.1 us
  blocking collectives  26 us (35%)
  waiting for transfers between devices  17.9 us (24%)
  Pallas kernels  14.3 us (19%)
  starting transfers between devices  12.6 us (17%)
  local copies, waits for them, and re-layouts  2.56 us (3%)
    all_to_all x1, blocking collectives, local(): received = lax.all_to_all(sent, AXES, 0, 0, axis_index_groups=alone)  23.9 us
    all_to_all x1, waiting for transfers between devices, local(): shares = lax.all_to_all(partial, AXES, 0, 0, axis_index_groups=paired)  16.5 us
    pallas_call x1, Pallas kernels, local(): pl.pallas_call(force_kernel, out_shape=jax.ShapeDtypeStruct((MEMBERS, 8,...  12.2 us
    all_to_all x1, starting transfers between devices, local(): shares = lax.all_to_all(partial, AXES, 0, 0, axis_index_groups=paired)  5.37 us
    ppermute x1, starting transfers between devices, local(): passed = lax.ppermute(slots, ('xh', 'xl'), [(x, 3 - x) for x in range(4)])  4.38 us
    ppermute x1, starting transfers between devices, local(): other = lax.ppermute(table, 'core', [(0, 1), (1, 0)])  2.86 us
    unnamed x8, local copies, waits for them, and re-layouts  2.56 us
    all_gather x1, blocking collectives, local(): halves = lax.all_gather(half_result, 'core')  2.08 us
  transfers between devices with their start and end apart: 3, of which 2 were waited for; matrix products, arithmetic and copies ran while one was open for 0% of the time, Pallas kernels for 1%

profile of v4, /device:TPU:449, one launch (start us, length us, event | category | flops | bytes accessed | tf_op | source)
XLA Modules:
  0.0 74.1 jit_solution(9582717713690580643)
XLA Ops:
  0.0 4.4 %collective-permute-start = (s32[8,128]{1,0:T(8,128)}, s32[8,128]{1,0:T(8,128)S(1)}, u32[]{:S(2)}, u32[]{:S(2)}) collective-permute-start(s32[8,128]{1,0:T(8,128)} %bitcast.13), channel_id=1, source_target_pairs={{0,24},{8,16},{16,8},{24,0},{1,25},{9,17},{17,9},{25,1},{2,26},{10... | collective-permute-start | bytes 12296 | tf_op jit(solution)/shard_map/ppermute | solution.py:243
  4.4 0.0 copy-start.1
  4.4 1.0 %copy-done.1 = f32[12,8192]{1,0:T(8,128)S(1)} copy-done((f32[12,8192]{1,0:T(8,128)S(1)}, f32[12,8192]{1,0:T(8,128)}, u32[]{:S(2)}) %copy-start.1) | copy-done | bytes 393240
  5.4 0.0 copy-start.2
  5.4 0.8 %copy-done.2 = f32[8192]{0:T(1024)S(1)} copy-done((f32[8192]{0:T(1024)S(1)}, f32[8192]{0:T(1024)}, u32[]{:S(2)}) %copy-start.2) | copy-done | bytes 32792
  6.2 0.0 copy-start.3
  6.2 0.8 %copy-done.3 = s32[8192]{0:T(1024)S(1)} copy-done((s32[8192]{0:T(1024)S(1)}, s32[8192]{0:T(1024)}, u32[]{:S(2)}) %copy-start.3) | copy-done | bytes 32792
  6.9 0.8 %table.1.mine = f32[16,8192]{1,0:T(8,128)S(1)} custom-call(f32[12,8192]{1,0:T(8,128)S(1)} %copy-done.1, f32[1,8192]{1,0:T(1,128)S(1)} %bitcast.15, s32[1,8192]{1,0:T(1,128)S(1)} %bitcast.16), custom_call_target="tpu_custom_call" | custom-call | flops 10000000000 | bytes 983040 | tf_op jit(solution)/shard_map/table/pallas_call | solution.py:245
  7.7 0.0 collective-permute-done.passed_slots
  7.7 2.9 %collective-permute-start.1 = (f32[16,8192]{1,0:T(8,128)S(1)}, f32[16,8192]{1,0:T(8,128)S(1)}, u32[]{:S(2)}, u32[]{:S(2)}) collective-permute-start(f32[16,8192]{1,0:T(8,128)S(1)} %table.1.mine), channel_id=1, source_target_pairs={{0,32},{32,0},{1,33},{33,1},{2,34},{34,2},{3,35},{35,3},{4,36},{36... | collective-permute-start | bytes 1572872 | tf_op jit(solution)/shard_map/ppermute | solution.py:263
  10.6 0.0 copy-start
  10.6 0.1 pad_add_fusion.where
  10.7 1.4 %collective-permute-done.1.other = f32[16,8192]{1,0:T(8,128)S(1)} collective-permute-done((f32[16,8192]{1,0:T(8,128)S(1)}, f32[16,8192]{1,0:T(8,128)S(1)}, u32[]{:S(2)}, u32[]{:S(2)}) %collective-permute-start.1) | collective-permute-done | bytes 524320 | tf_op jit(solution)/shard_map/ppermute | solution.py:263
  12.1 0.0 copy-done
  12.1 1.3 %lookup.1 = f32[8,16,256]{2,1,0:T(8,128)S(1)} custom-call(s32[4]{0:T(128)S(1)} %pad_add_fusion.where, s32[8,128]{1,0:T(8,128)S(1)} %bitcast.14, s32[8,128]{1,0:T(8,128)S(1)} %collective-permute-done.passed_slots, f32[16,8192]{1,0:T(8,128)S(1)} %table.1.mine, f32[16,8192]{1,0:T(8,128)S(1)} %collective-permute-done.1.other), custom_call_target="tpu_custom_call" | custom-call | tf_op jit(solution)/shard_map/lookup/pallas_call | solution.py:264
  13.4 23.9 %all_to_all.10.received = f32[8,16,256]{2,1,0:T(8,128)S(1)} all-to-all(f32[8,16,256]{2,1,0:T(8,128)S(1)} %lookup.1), channel_id=1, replica_groups={{320,192,448,64,256,128,384,0},{321,193,449,65,257,129,385,1},{322,194,..., dimensions={0} | all-to-all | bytes 262144 | tf_op jit(solution)/shard_map/all_to_all | solution.py:273
  37.3 12.2 %forces.1 = f32[16,8,256]{2,1,0:T(8,128)} custom-call(s32[4]{0:T(128)S(1)} %pad_add_fusion.where, f32[8,16,256]{2,1,0:T(8,128)S(1)} %all_to_all.10.received, f32[16,8192]{1,0:T(8,128)S(1)} %table.1.mine, f32[16,8192]{1,0:T(8,128)S(1)} %collective-permute-done.1.other), custom_call_target="tpu_custom_call" | custom-call | tf_op jit(solution)/shard_map/forces/pallas_call | solution.py:274
  49.5 5.4 %all-to-all-start.1 = ((f32[16,8,256]{2,1,0:T(8,128)}), f32[16,8,256]{2,1,0:T(8,128)S(1)}, u32[]{:S(2)}, u32[]{:S(2)}) async-start(f32[16,8,256]{2,1,0:T(8,128)} %forces.1), calls=%async_computation.1 | async-start | bytes 262144 | tf_op jit(solution)/shard_map/all_to_all | solution.py:290
  54.9 16.5 %all-to-all-done.1.received = f32[16,8,256]{2,1,0:T(8,128)S(1)} async-done(((f32[16,8,256]{2,1,0:T(8,128)}), f32[16,8,256]{2,1,0:T(8,128)S(1)}, u32[]{:S(2)}, u32[]{:S(2)}) %all-to-all-start.1) | async-done | bytes 131104 | tf_op jit(solution)/shard_map/all_to_all | solution.py:290
  71.4 2.1 %all-gather.1 = f32[2,12,512]{2,1,0:T(8,128)S(1)} all-gather(f32[1,12,512]{2,1,0:T(8,128)S(1)} %bitcast.12), channel_id=2, replica_groups=mesh['y'=4,'zh'=2,'core'=2,'xh'=2,'xl'=2,'zl'=8] {'core'}, dimensions={0}, use_global_device_ids=true | all-gather | bytes 73728 | tf_op jit(solution)/shard_map/all_gather | solution.py:299
  73.5 0.6 maximum_select_fusion
  (3 shorter events, 0.0 us)
Async XLA Ops:
  0.0 7.7 %collective-permute-start = (s32[8,128]{1,0:T(8,128)}, s32[8,128]{1,0:T(8,128)S(1)}, u32[]{:S(2)}, u32[]{:S(2)}) collective-permute-start(s32[8,128]{1,0:T(8,128)} %bitcast.13), channel_id=1, source_target_pairs={{0,24},{8,16},{16,8},{24,0},{1,25},{9,17},{17,9},{25,1},{2,26},{10... | collective-permute-start | bytes 12296 | tf_op jit(solution)/shard_map/ppermute | solution.py:243
  4.4 1.0 %copy-start.1 = (f32[12,8192]{1,0:T(8,128)S(1)}, f32[12,8192]{1,0:T(8,128)}, u32[]{:S(2)}) copy-start(f32[12,8192]{1,0:T(8,128)} %state_in.1) | copy-start | bytes 1179652
  5.4 0.8 %copy-start.2 = (f32[8192]{0:T(1024)S(1)}, f32[8192]{0:T(1024)}, u32[]{:S(2)}) copy-start(f32[8192]{0:T(1024)} %param.5) | copy-start | bytes 98308
  6.2 0.8 %copy-start.3 = (s32[8192]{0:T(1024)S(1)}, s32[8192]{0:T(1024)}, u32[]{:S(2)}) copy-start(s32[8192]{0:T(1024)} %param.6) | copy-start | bytes 98308
  7.7 4.4 %collective-permute-start.1 = (f32[16,8192]{1,0:T(8,128)S(1)}, f32[16,8192]{1,0:T(8,128)S(1)}, u32[]{:S(2)}, u32[]{:S(2)}) collective-permute-start(f32[16,8192]{1,0:T(8,128)S(1)} %table.1.mine), channel_id=1, source_target_pairs={{0,32},{32,0},{1,33},{33,1},{2,34},{34,2},{3,35},{35,3},{4,36},{36... | collective-permute-start | bytes 1572872 | tf_op jit(solution)/shard_map/ppermute | solution.py:263
  10.6 1.5 %copy-start = (s32[1024]{0:T(1024)S(1)}, s32[1024]{0:T(1024)}, u32[]{:S(2)}) copy-start(s32[1024]{0:T(1024)} %param.7) | copy-start | bytes 12292
  49.5 21.9 %all-to-all-start.1 = ((f32[16,8,256]{2,1,0:T(8,128)}), f32[16,8,256]{2,1,0:T(8,128)S(1)}, u32[]{:S(2)}, u32[]{:S(2)}) async-start(f32[16,8,256]{2,1,0:T(8,128)} %forces.1), calls=%async_computation.1 | async-start | bytes 262144 | tf_op jit(solution)/shard_map/all_to_all | solution.py:290

commit v5 on v4

--- a/solution.py
+++ b/solution.py
@@ -25,10 +25,12 @@
 NEAR = 8
 Y_ORDER = (2, 1, 3, 0)
 CHUNK = 512
+UNROLL = 16
 SOURCES = 2 * SHARD
 FULL = pl.BlockSpec(memory_space=pltpu.VMEM)
 SCALARS = pl.BlockSpec(memory_space=pltpu.SMEM)
 PARAMS = pltpu.CompilerParams(vmem_limit_bytes=48 * 2**20)
+LONG = pl.CostEstimate(flops=10**10, bytes_accessed=2**24, transcendentals=0)
 NN = (((1,), (0,)), ((), ()))
 TN = (((0,), (0,)), ((), ()))
 dot = functools.partial(lax.dot_general, preferred_element_type=f32)
@@ -70,6 +72,17 @@
 def high_low(value):
     high = value.astype(bf16)
     return high, (value - high.astype(f32)).astype(bf16)
+
+
+def slots_kernel(slots_in, slots):
+    slots[...] = slots_in[...]
+
+
+def index_kernel(where, own_slots, passed_slots, index):
+    core, helper = where[1], where[2]
+    at = pl.ds(core * 4 + helper * 2, 2)
+    chosen = jnp.where(helper == 0, own_slots[at, :], passed_slots[at, :])
+    index[...] = jnp.concatenate((chosen[0:1], chosen[1:2]), 1)
 
 
 def table_kernel(state_in, mass_in, level_in, table, state, mass, level, done):
@@ -100,11 +113,9 @@
     table[15:16, :] = 3.0 * jnp.sum(place * speed, 0, keepdims=True)
 
 
-def lookup_kernel(where, own_slots, passed_slots, mine, other, out):
-    first, core, helper = where[0], where[1], where[2]
-    at = pl.ds(core * 4 + helper * 2, 2)
-    index = jnp.where(helper == 0, own_slots[at, :], passed_slots[at, :])
-    index = jnp.concatenate((index[0:1], index[1:2]), 1)
+def lookup_kernel(where, index_in, mine, other, out):
+    first, core = where[0], where[1]
+    index = index_in[...]
     picked = jnp.zeros((16, PART), f32)
     for table, start in ((mine, first + core * SHARD), (other, first + (1 - core) * SHARD)):
         local_index = index - start
@@ -125,29 +136,20 @@
         out[member] = picked
 
 
-def source_features(table, features, pull, swing, offset):
-    def step(turn, _):
-        at = pl.ds(pl.multiple_of(turn * CHUNK, CHUNK), CHUNK)
-        to = pl.ds(pl.multiple_of(offset + turn * CHUNK, CHUNK), CHUNK)
-        upper, lower = table[0:8, at], table[8:16, at]
-        row = rows_of(upper)
-        a, b, c = split(jnp.where(row == 7, 1.0, upper))
-        d, e, f = split(lower)
-        zero = jnp.zeros_like(a)
-        pairs = ((a, a), (a, b), (b, c), (d, e), (f, zero))
-        for k, pair in enumerate(pairs):
-            features[16 * k : 16 * k + 16, to] = jnp.concatenate(pair, 0).astype(bf16)
-        weight = upper[6:7] * (1.0 / STARS)
-        moved = jnp.where(row == 7, 0.0, jnp.where(row == 6, 1.0, upper)) * weight
-        placed = pltpu.roll(moved, 3, 0)
-        turned = jnp.where(row == 7, weight, jnp.where((row >= 3) & (row < 6), -placed, 0.0))
-        for ref, value in ((pull, moved), (swing, turned)):
-            a, b, c = split(value)
-            ref[0:16, to] = jnp.concatenate((a, b), 0).astype(bf16)
-            ref[16:32, to] = jnp.concatenate((c, zero), 0).astype(bf16)
-        return 0
-
-    lax.fori_loop(0, SHARD // CHUNK, step, 0)
+def source_features(upper, lower):
+    row = rows_of(upper)
+    a, b, c = split(jnp.where(row == 7, 1.0, upper))
+    d, e, f = split(lower)
+    zero = jnp.zeros_like(a)
+    features = jnp.concatenate((a, a, a, b, b, c, d, e, f, zero), 0).astype(bf16)
+    weight = upper[6:7] * (1.0 / STARS)
+    moved = jnp.where(row == 7, 0.0, jnp.where(row == 6, 1.0, upper)) * weight
+    placed = pltpu.roll(moved, 3, 0)
+    turned = jnp.where(row == 7, weight, jnp.where((row >= 3) & (row < 6), -placed, 0.0))
+    pull, swing = [
+        jnp.concatenate(split(value) + (zero,), 0).astype(bf16) for value in (moved, turned)
+    ]
+    return features, pull, swing
 
 
 def target_features(target):
@@ -174,35 +176,33 @@
     return result
 
 
-def force_kernel(where, received, mine, other, out, features, pull, swing, total, rows):
+def force_kernel(where, received, mine, other, out, total, rows):
     target_rows = received[0]
     for sender in range(1, SENDERS):
         target_rows = target_rows + received[sender]
     target = target_rows[0:8]
     rows[...] = target_rows
-    source_features(mine, features, pull, swing, 0)
-    source_features(other, features, pull, swing, SHARD)
     radius_part, near_part = target_features(target)
     total[...] = jnp.zeros_like(total)
-
-    def step(turn, _):
-        at = pl.ds(pl.multiple_of(turn * CHUNK, CHUNK), CHUNK)
-        source = features[:, at]
-        radius_sq = dot(source, radius_part, TN)
-        product = dot(source, near_part, TN)
-        inverse = lax.rsqrt(radius_sq)
-        inverse_sq = inverse * inverse
-        strength = inverse_sq * inverse
-        turning = (product * inverse_sq) * strength
-        pulls, swings = pull[:, at], swing[:, at]
-        total[...] += dot(
-            jnp.concatenate((pulls, pulls, swings, swings), 1),
-            jnp.concatenate(high_low(strength) + high_low(turning), 0),
-            NN,
-        )
-        return 0
-
-    lax.fori_loop(0, SOURCES // CHUNK, step, 0, unroll=16)
+    for table in (mine, other):
+
+        def step(turn, _):
+            at = pl.ds(pl.multiple_of(turn * CHUNK, CHUNK), CHUNK)
+            source, pull, swing = source_features(table[0:8, at], table[8:16, at])
+            radius_sq = dot(source, radius_part, TN)
+            product = dot(source, near_part, TN)
+            inverse = lax.rsqrt(radius_sq)
+            inverse_sq = inverse * inverse
+            strength = inverse_sq * inverse
+            turning = (product * inverse_sq) * strength
+            total[...] += dot(
+                jnp.concatenate((pull, pull, swing, swing), 1),
+                jnp.concatenate(high_low(strength) + high_low(turning), 0),
+                NN,
+            )
+            return 0
+
+        lax.fori_loop(0, SHARD // CHUNK, step, 0, unroll=UNROLL)
     sums = total[0:8] + total[8:16] + total[16:24]
     place, speed = target[0:3], target[3:6]
     accel = sums[0:3] - place * sums[6:7]
@@ -239,7 +239,15 @@
     y, zh = lax.axis_index("y"), lax.axis_index("zh")
     sender = sender_of(y, zh, lax.axis_index("zl"))
     where = jnp.stack([(y * 2 + zh) * SOURCES, core, helper, sender]).astype(jnp.int32)
-    slots = active_slots.reshape(8, 128)
+    slots = pl.pallas_call(
+        slots_kernel,
+        out_shape=jax.ShapeDtypeStruct((8, 128), jnp.int32),
+        in_specs=[FULL],
+        out_specs=FULL,
+        compiler_params=PARAMS,
+        cost_estimate=LONG,
+        name="slots",
+    )(active_slots.reshape(8, 128))
     passed = lax.ppermute(slots, ("xh", "xl"), [(x, 3 - x) for x in range(4)])
     anywhere = pl.BlockSpec(memory_space=pl.ANY)
     table = pl.pallas_call(
@@ -254,21 +262,27 @@
             pltpu.SemaphoreType.DMA((3,)),
         ],
         compiler_params=PARAMS,
-        cost_estimate=pl.CostEstimate(
-            flops=10**10, bytes_accessed=120 * SHARD, transcendentals=0
-        ),
+        cost_estimate=LONG,
         name="table",
     )(star_state, star_mass.reshape(1, SHARD), star_level.reshape(1, SHARD))
-    table, passed = lax.optimization_barrier((table, passed))
     other = lax.ppermute(table, "core", [(0, 1), (1, 0)])
+    index = pl.pallas_call(
+        index_kernel,
+        out_shape=jax.ShapeDtypeStruct((1, PART), jnp.int32),
+        in_specs=[SCALARS] + [FULL] * 2,
+        out_specs=FULL,
+        compiler_params=PARAMS,
+        cost_estimate=LONG,
+        name="index",
+    )(where, slots, passed)
     sent = pl.pallas_call(
         lookup_kernel,
         out_shape=jax.ShapeDtypeStruct((SENDERS, 16, PART), f32),
-        in_specs=[SCALARS] + [FULL] * 4,
+        in_specs=[SCALARS] + [FULL] * 3,
         out_specs=FULL,
         compiler_params=PARAMS,
         name="lookup",
-    )(where, slots, passed, table, other)
+    )(where, index, table, other)
     alone = exchange_groups([(x,) for x in range(4)])
     received = lax.all_to_all(sent, AXES, 0, 0, axis_index_groups=alone)
     partial = pl.pallas_call(
@@ -277,9 +291,6 @@
         in_specs=[SCALARS] + [FULL] * 3,
         out_specs=FULL,
         scratch_shapes=[
-            pltpu.VMEM((80, SOURCES), bf16),
-            pltpu.VMEM((32, SOURCES), bf16),
-            pltpu.VMEM((32, SOURCES), bf16),
             pltpu.VMEM((32, PART), f32),
             pltpu.VMEM((16, PART), f32),
         ],

time: 74.6 us -> 71.5 us (0.958)
  local copies, waits for them, and re-layouts: 2.56 us -> 0.71 us
  Pallas kernels: 14.3 us -> 13.4 us
    unnamed x8 -> x10, local copies, waits for them, and re-layouts: 2.56 us -> 0.7 us
    pallas_call x1, Pallas kernels: 12.2 us -> 10.8 us  [local(): pl.pallas_call(force_kernel, out_shape=jax.ShapeDtypeStruct((MEMBERS, 8,...]
  transfers between devices with their start and end apart: 3 -> 3, of which waited for: 2 -> 2; matrix products, arithmetic and copies ran while one was open for 0% -> 0% of each run, Pallas kernels for 1% -> 2%
where the time goes in v5:
time: 71.5 us; the launch traced here: 71.2 us
  blocking collectives  26 us (36%)
  waiting for transfers between devices  17.3 us (24%)
  Pallas kernels  13.4 us (19%)
  starting transfers between devices  12.9 us (18%)
  other arithmetic  0.72 us (1%)
    all_to_all x1, blocking collectives, local(): received = lax.all_to_all(sent, AXES, 0, 0, axis_index_groups=alone)  23.9 us
    all_to_all x1, waiting for transfers between devices, local(): shares = lax.all_to_all(partial, AXES, 0, 0, axis_index_groups=paired)  16.5 us
    pallas_call x1, Pallas kernels, local(): pl.pallas_call(force_kernel, out_shape=jax.ShapeDtypeStruct((MEMBERS, 8,...  10.8 us
    all_to_all x1, starting transfers between devices, local(): shares = lax.all_to_all(partial, AXES, 0, 0, axis_index_groups=paired)  5.5 us
    ppermute x1, starting transfers between devices, local(): passed = lax.ppermute(slots, ('xh', 'xl'), [(x, 3 - x) for x in range(4)])  4.52 us
    ppermute x1, starting transfers between devices, local(): other = lax.ppermute(table, 'core', [(0, 1), (1, 0)])  2.86 us
    all_gather x1, blocking collectives, local(): halves = lax.all_gather(half_result, 'core')  2.07 us
  transfers between devices with their start and end apart: 3, of which 2 were waited for; matrix products, arithmetic and copies ran while one was open for 0% of the time, Pallas kernels for 2%

profile of v5, /device:TPU:449, one launch (start us, length us, event | category | flops | bytes accessed | tf_op | source)
XLA Modules:
  0.0 71.2 jit_solution(1889834834549549683)
XLA Ops:
  0.0 0.0 copy-start
  0.0 0.7 copy-done
  0.7 0.0 copy-start.2
  0.7 0.0 copy-start.3
  0.7 0.0 copy-start.4
  0.7 4.5 %collective-permute-start = (s32[8,128]{1,0:T(8,128)S(1)}, s32[8,128]{1,0:T(8,128)S(1)}, u32[]{:S(2)}, u32[]{:S(2)}) collective-permute-start(s32[8,128]{1,0:T(8,128)S(1)} %slots.1.own_slots), channel_id=1, source_target_pairs={{0,24},{8,16},{16,8},{24,0},{1,25},{9,17},{17,9},{25,1},{2,26},{10... | collective-permute-start | bytes 12296 | tf_op jit(solution)/shard_map/ppermute | solution.py:251
  5.2 0.0 copy-done.2
  5.2 0.0 copy-done.3
  5.2 0.0 copy-done.4
  5.3 0.8 %table.1.mine = f32[16,8192]{1,0:T(8,128)S(1)} custom-call(f32[12,8192]{1,0:T(8,128)S(1)} %copy-done.2, f32[1,8192]{1,0:T(1,128)S(1)} %bitcast.14, s32[1,8192]{1,0:T(1,128)S(1)} %bitcast.15), custom_call_target="tpu_custom_call" | custom-call | flops 10000000000 | bytes 16777216 | tf_op jit(solution)/shard_map/table/pallas_call | solution.py:253
  6.0 2.9 %collective-permute-start.1 = (f32[16,8192]{1,0:T(8,128)S(1)}, f32[16,8192]{1,0:T(8,128)S(1)}, u32[]{:S(2)}, u32[]{:S(2)}) collective-permute-start(f32[16,8192]{1,0:T(8,128)S(1)} %table.1.mine), channel_id=1, source_target_pairs={{0,32},{32,0},{1,33},{33,1},{2,34},{34,2},{3,35},{35,3},{4,36},{36... | collective-permute-start | bytes 1572872 | tf_op jit(solution)/shard_map/ppermute | solution.py:268
  8.9 0.1 pad_add_fusion.where
  9.0 0.0 collective-permute-done.passed_slots
  9.0 0.6 index.1.index_in
  9.6 0.8 %collective-permute-done.1.other = f32[16,8192]{1,0:T(8,128)S(1)} collective-permute-done((f32[16,8192]{1,0:T(8,128)S(1)}, f32[16,8192]{1,0:T(8,128)S(1)}, u32[]{:S(2)}, u32[]{:S(2)}) %collective-permute-start.1) | collective-permute-done | bytes 524320 | tf_op jit(solution)/shard_map/ppermute | solution.py:268
  10.4 1.3 %lookup.1 = f32[8,16,256]{2,1,0:T(8,128)S(1)} custom-call(s32[4]{0:T(128)S(1)} %pad_add_fusion.where, s32[1,256]{1,0:T(1,128)S(1)} %index.1.index_in, f32[16,8192]{1,0:T(8,128)S(1)} %table.1.mine, f32[16,8192]{1,0:T(8,128)S(1)} %collective-permute-done.1.other), custom_call_target="tpu_custom_call" | custom-call | tf_op jit(solution)/shard_map/lookup/pallas_call | solution.py:278
  11.7 23.9 %all_to_all.10.received = f32[8,16,256]{2,1,0:T(8,128)S(1)} all-to-all(f32[8,16,256]{2,1,0:T(8,128)S(1)} %lookup.1), channel_id=1, replica_groups={{320,192,448,64,256,128,384,0},{321,193,449,65,257,129,385,1},{322,194,..., dimensions={0} | all-to-all | bytes 262144 | tf_op jit(solution)/shard_map/all_to_all | solution.py:287
  35.6 10.8 %forces.1 = f32[16,8,256]{2,1,0:T(8,128)} custom-call(s32[4]{0:T(128)S(1)} %pad_add_fusion.where, f32[8,16,256]{2,1,0:T(8,128)S(1)} %all_to_all.10.received, f32[16,8192]{1,0:T(8,128)S(1)} %table.1.mine, f32[16,8192]{1,0:T(8,128)S(1)} %collective-permute-done.1.other), custom_call_target="tpu_custom_call" | custom-call | tf_op jit(solution)/shard_map/forces/pallas_call | solution.py:288
  46.4 0.0 copy-start.1
  46.4 5.5 %all-to-all-start.1 = ((f32[16,8,256]{2,1,0:T(8,128)}), f32[16,8,256]{2,1,0:T(8,128)S(1)}, u32[]{:S(2)}, u32[]{:S(2)}) async-start(f32[16,8,256]{2,1,0:T(8,128)} %forces.1), calls=%async_computation.1 | async-start | bytes 262144 | tf_op jit(solution)/shard_map/all_to_all | solution.py:301
  51.9 0.0 copy-done.1
  52.0 16.5 %all-to-all-done.1.received = f32[16,8,256]{2,1,0:T(8,128)S(1)} async-done(((f32[16,8,256]{2,1,0:T(8,128)}), f32[16,8,256]{2,1,0:T(8,128)S(1)}, u32[]{:S(2)}, u32[]{:S(2)}) %all-to-all-start.1) | async-done | bytes 131104 | tf_op jit(solution)/shard_map/all_to_all | solution.py:301
  68.4 2.1 %all-gather.1 = f32[2,12,512]{2,1,0:T(8,128)S(1)} all-gather(f32[1,12,512]{2,1,0:T(8,128)S(1)} %bitcast.12), channel_id=2, replica_groups=mesh['y'=4,'zh'=2,'core'=2,'xh'=2,'xl'=2,'zl'=8] {'core'}, dimensions={0}, use_global_device_ids=true | all-gather | bytes 73728 | tf_op jit(solution)/shard_map/all_gather | solution.py:310
  70.5 0.6 maximum_select_fusion
  (4 shorter events, 0.0 us)
Async XLA Ops:
  0.0 0.7 copy-start
  0.7 4.5 %copy-start.2 = (f32[12,8192]{1,0:T(8,128)S(1)}, f32[12,8192]{1,0:T(8,128)}, u32[]{:S(2)}) copy-start(f32[12,8192]{1,0:T(8,128)} %state_in.1) | copy-start | bytes 1179652
  0.7 4.5 %copy-start.3 = (f32[8192]{0:T(1024)S(1)}, f32[8192]{0:T(1024)}, u32[]{:S(2)}) copy-start(f32[8192]{0:T(1024)} %param.5) | copy-start | bytes 98308
  0.7 4.6 %copy-start.4 = (s32[8192]{0:T(1024)S(1)}, s32[8192]{0:T(1024)}, u32[]{:S(2)}) copy-start(s32[8192]{0:T(1024)} %param.6) | copy-start | bytes 98308
  0.7 8.3 %collective-permute-start = (s32[8,128]{1,0:T(8,128)S(1)}, s32[8,128]{1,0:T(8,128)S(1)}, u32[]{:S(2)}, u32[]{:S(2)}) collective-permute-start(s32[8,128]{1,0:T(8,128)S(1)} %slots.1.own_slots), channel_id=1, source_target_pairs={{0,24},{8,16},{16,8},{24,0},{1,25},{9,17},{17,9},{25,1},{2,26},{10... | collective-permute-start | bytes 12296 | tf_op jit(solution)/shard_map/ppermute | solution.py:251
  6.0 4.4 %collective-permute-start.1 = (f32[16,8192]{1,0:T(8,128)S(1)}, f32[16,8192]{1,0:T(8,128)S(1)}, u32[]{:S(2)}, u32[]{:S(2)}) collective-permute-start(f32[16,8192]{1,0:T(8,128)S(1)} %table.1.mine), channel_id=1, source_target_pairs={{0,32},{32,0},{1,33},{33,1},{2,34},{34,2},{3,35},{35,3},{4,36},{36... | collective-permute-start | bytes 1572872 | tf_op jit(solution)/shard_map/ppermute | solution.py:268
  46.4 5.5 %copy-start.1 = (s32[1024]{0:T(1024)S(1)}, s32[1024]{0:T(1024)}, u32[]{:S(2)}) copy-start(s32[1024]{0:T(1024)} %param.7) | copy-start | bytes 12292
  46.4 22.0 %all-to-all-start.1 = ((f32[16,8,256]{2,1,0:T(8,128)}), f32[16,8,256]{2,1,0:T(8,128)S(1)}, u32[]{:S(2)}, u32[]{:S(2)}) async-start(f32[16,8,256]{2,1,0:T(8,128)} %forces.1), calls=%async_computation.1 | async-start | bytes 262144 | tf_op jit(solution)/shard_map/all_to_all | solution.py:301

commit v6 on v5

--- a/solution.py
+++ b/solution.py
@@ -18,6 +18,7 @@
 BLK = ("y", "zh", "core")
 ACT = ("xh", "xl", "zl")
 SHARD = 8192
+ROWS = 15
 HALF = 512
 PART = 256
 SENDERS = 8
@@ -76,13 +77,6 @@
 
 def slots_kernel(slots_in, slots):
     slots[...] = slots_in[...]
-
-
-def index_kernel(where, own_slots, passed_slots, index):
-    core, helper = where[1], where[2]
-    at = pl.ds(core * 4 + helper * 2, 2)
-    chosen = jnp.where(helper == 0, own_slots[at, :], passed_slots[at, :])
-    index[...] = jnp.concatenate((chosen[0:1], chosen[1:2]), 1)
 
 
 def table_kernel(state_in, mass_in, level_in, table, state, mass, level, done):
@@ -110,24 +104,26 @@
     table[8:11, :] = x + half * v + step_sq * a
     table[11:14, :] = v + half * a + step_sq * j
     table[14:15, :] = jnp.sum(place * place, 0, keepdims=True)
-    table[15:16, :] = 3.0 * jnp.sum(place * speed, 0, keepdims=True)
-
-
-def lookup_kernel(where, index_in, mine, other, out):
-    first, core = where[0], where[1]
-    index = index_in[...]
+
+
+def lookup_kernel(where, own_slots, passed_slots, tables, out):
+    first, core, helper = where[0], where[1], where[2]
+    at = pl.ds(core * 4 + helper * 2, 2)
+    index = jnp.where(helper == 0, own_slots[at, :], passed_slots[at, :])
+    index = jnp.concatenate((index[0:1], index[1:2]), 1)
     picked = jnp.zeros((16, PART), f32)
-    for table, start in ((mine, first + core * SHARD), (other, first + (1 - core) * SHARD)):
-        local_index = index - start
+    spare = jnp.zeros((16 - ROWS, 128), f32)
+    for k in range(2):
+        local_index = index - (first + k * SHARD)
         low, high = local_index & 127, local_index >> 7
         low = jnp.broadcast_to(low, (128, PART))
         hit = jnp.where(rows_of(low) == low, 1.0, 0.0).astype(bf16)
         hits = jnp.concatenate((hit, hit, hit), 0)
         high = jnp.broadcast_to(high, (16, PART))
         for block in range(SHARD // 2048):
-            tiles = [
-                table[:, (block * 16 + i) * 128 : (block * 16 + i + 1) * 128] for i in range(16)
-            ]
+            tiles = []
+            for i in range(block * 16, block * 16 + 16):
+                tiles += [tables[k, :, i * 128 : (i + 1) * 128], spare]
             parts = [part.astype(bf16) for part in split(jnp.concatenate(tiles, 0))]
             found = dot(jnp.concatenate(parts, 1), hits, NN)
             for i in range(16):
@@ -136,10 +132,12 @@
         out[member] = picked
 
 
-def source_features(upper, lower):
+def source_features(upper, place_sq):
     row = rows_of(upper)
+    speed = pltpu.roll(upper, 5, 0)
+    product = 3.0 * jnp.sum(jnp.where(row < 3, upper * speed, 0.0), 0, keepdims=True)
     a, b, c = split(jnp.where(row == 7, 1.0, upper))
-    d, e, f = split(lower)
+    d, e, f = split(jnp.where(row == 6, place_sq, jnp.where(row == 7, product, 0.0)))
     zero = jnp.zeros_like(a)
     features = jnp.concatenate((a, a, a, b, b, c, d, e, f, zero), 0).astype(bf16)
     weight = upper[6:7] * (1.0 / STARS)
@@ -176,7 +174,7 @@
     return result
 
 
-def force_kernel(where, received, mine, other, out, total, rows):
+def force_kernel(where, received, tables, out, total, rows):
     target_rows = received[0]
     for sender in range(1, SENDERS):
         target_rows = target_rows + received[sender]
@@ -184,11 +182,11 @@
     rows[...] = target_rows
     radius_part, near_part = target_features(target)
     total[...] = jnp.zeros_like(total)
-    for table in (mine, other):
-
-        def step(turn, _):
+    for k in range(2):
+
+        def step(turn, _, k=k):
             at = pl.ds(pl.multiple_of(turn * CHUNK, CHUNK), CHUNK)
-            source, pull, swing = source_features(table[0:8, at], table[8:16, at])
+            source, pull, swing = source_features(tables[k, 0:8, at], tables[k, 14:15, at])
             radius_sq = dot(source, radius_part, TN)
             product = dot(source, near_part, TN)
             inverse = lax.rsqrt(radius_sq)
@@ -252,7 +250,7 @@
     anywhere = pl.BlockSpec(memory_space=pl.ANY)
     table = pl.pallas_call(
         table_kernel,
-        out_shape=jax.ShapeDtypeStruct((16, SHARD), f32),
+        out_shape=jax.ShapeDtypeStruct((ROWS, SHARD), f32),
         in_specs=[anywhere] * 3,
         out_specs=FULL,
         scratch_shapes=[
@@ -265,16 +263,7 @@
         cost_estimate=LONG,
         name="table",
     )(star_state, star_mass.reshape(1, SHARD), star_level.reshape(1, SHARD))
-    other = lax.ppermute(table, "core", [(0, 1), (1, 0)])
-    index = pl.pallas_call(
-        index_kernel,
-        out_shape=jax.ShapeDtypeStruct((1, PART), jnp.int32),
-        in_specs=[SCALARS] + [FULL] * 2,
-        out_specs=FULL,
-        compiler_params=PARAMS,
-        cost_estimate=LONG,
-        name="index",
-    )(where, slots, passed)
+    tables = lax.all_gather(table, "core")
     sent = pl.pallas_call(
         lookup_kernel,
         out_shape=jax.ShapeDtypeStruct((SENDERS, 16, PART), f32),
@@ -282,13 +271,13 @@
         out_specs=FULL,
         compiler_params=PARAMS,
         name="lookup",
-    )(where, index, table, other)
+    )(where, slots, passed, tables)
     alone = exchange_groups([(x,) for x in range(4)])
     received = lax.all_to_all(sent, AXES, 0, 0, axis_index_groups=alone)
     partial = pl.pallas_call(
         force_kernel,
         out_shape=jax.ShapeDtypeStruct((MEMBERS, 8, PART), f32),
-        in_specs=[SCALARS] + [FULL] * 3,
+        in_specs=[SCALARS] + [FULL] * 2,
         out_specs=FULL,
         scratch_shapes=[
             pltpu.VMEM((32, PART), f32),
@@ -296,7 +285,7 @@
         ],
         compiler_params=PARAMS,
         name="forces",
-    )(where, received, table, other)
+    )(where, received, tables)
     paired = exchange_groups([(x, 3 - x) for x in range(2)])
     shares = lax.all_to_all(partial, AXES, 0, 0, axis_index_groups=paired)
     half_result = pl.pallas_call(

time: 71.5 us -> 70.2 us (0.982)
  blocking collectives: 26 us -> 29.1 us
  starting transfers between devices: 12.9 us -> 10 us
  waiting for transfers between devices: 17.3 us -> 16.5 us
    all_gather x0 -> x1, blocking collectives: none -> 3.14 us  [local(): tables = lax.all_gather(table, 'core')]
    ppermute x1 -> x0, starting transfers between devices: 2.86 us -> none  [local(): other = lax.ppermute(table, 'core', [(0, 1), (1, 0)])]
    ppermute x1 -> x0, waiting for transfers between devices: 0.85 us -> none  [local(): other = lax.ppermute(table, 'core', [(0, 1), (1, 0)])]
  transfers between devices with their start and end apart: 3 -> 2, of which waited for: 2 -> 1; matrix products, arithmetic and copies ran while one was open for 0% -> 0% of each run, Pallas kernels for 2% -> 1%
where the time goes in v6:
time: 70.2 us; the launch traced here: 69.9 us
  blocking collectives  29.1 us (41%)
  waiting for transfers between devices  16.5 us (24%)
  Pallas kernels  12.8 us (18%)
  starting transfers between devices  10 us (14%)
  other arithmetic  0.72 us (1%)
  local copies, waits for them, and re-layouts  0.71 us (1%)
    all_to_all x1, blocking collectives, local(): received = lax.all_to_all(sent, AXES, 0, 0, axis_index_groups=alone)  23.9 us
    all_to_all x1, waiting for transfers between devices, local(): shares = lax.all_to_all(partial, AXES, 0, 0, axis_index_groups=paired)  16.5 us
    pallas_call x1, Pallas kernels, local(): pl.pallas_call(force_kernel, out_shape=jax.ShapeDtypeStruct((MEMBERS, 8,...  10.7 us
    all_to_all x1, starting transfers between devices, local(): shares = lax.all_to_all(partial, AXES, 0, 0, axis_index_groups=paired)  5.5 us
    ppermute x1, starting transfers between devices, local(): passed = lax.ppermute(slots, ('xh', 'xl'), [(x, 3 - x) for x in range(4)])  4.52 us
    all_gather x1, blocking collectives, local(): tables = lax.all_gather(table, 'core')  3.14 us
    all_gather x1, blocking collectives, local(): halves = lax.all_gather(half_result, 'core')  2.07 us
  transfers between devices with their start and end apart: 2, of which 1 were waited for; matrix products, arithmetic and copies ran while one was open for 0% of the time, Pallas kernels for 1%

profile of v6, /device:TPU:449, one launch (start us, length us, event | category | flops | bytes accessed | tf_op | source)
XLA Modules:
  0.0 69.9 jit_solution(2906954254939738435)
XLA Ops:
  0.0 0.0 copy-start
  0.0 0.7 copy-done
  0.7 0.0 copy-start.2
  0.7 0.0 copy-start.4
  0.7 0.0 copy-start.3
  0.7 4.5 %collective-permute-start = (s32[8,128]{1,0:T(8,128)S(1)}, s32[8,128]{1,0:T(8,128)S(1)}, u32[]{:S(2)}, u32[]{:S(2)}) collective-permute-start(s32[8,128]{1,0:T(8,128)S(1)} %slots.1.own_slots), channel_id=1, source_target_pairs={{0,24},{8,16},{16,8},{24,0},{1,25},{9,17},{17,9},{25,1},{2,26},{10... | collective-permute-start | bytes 12296 | tf_op jit(solution)/shard_map/ppermute | solution.py:249
  5.2 0.0 copy-done.2
  5.3 0.0 copy-done.4
  5.3 0.0 copy-done.3
  5.3 0.7 table.1
  6.0 3.1 %all-gather.2.tables = f32[2,15,8192]{2,1,0:T(8,128)S(1)} all-gather(f32[1,15,8192]{2,1,0:T(8,128)S(1)} %bitcast.13), channel_id=2, replica_groups=mesh['y'=4,'zh'=2,'core'=2,'xh'=2,'xl'=2,'zl'=8] {'core'}, dimensions={0}, use_global_device_ids=true | all-gather | bytes 1474560 | tf_op jit(solution)/shard_map/all_gather | solution.py:266
  9.1 0.1 pad_add_fusion.where
  9.2 0.0 collective-permute-done.passed_slots
  9.2 1.3 %lookup.1 = f32[8,16,256]{2,1,0:T(8,128)S(1)} custom-call(s32[4]{0:T(128)S(1)} %pad_add_fusion.where, s32[8,128]{1,0:T(8,128)S(1)} %slots.1.own_slots, s32[8,128]{1,0:T(8,128)S(1)} %collective-permute-done.passed_slots, f32[2,15,8192]{2,1,0:T(8,128)S(1)} %all-gather.2.tables), custom_call_target="tpu_custom_call" | custom-call | tf_op jit(solution)/shard_map/lookup/pallas_call | solution.py:267
  10.5 23.9 %all_to_all.10.received = f32[8,16,256]{2,1,0:T(8,128)S(1)} all-to-all(f32[8,16,256]{2,1,0:T(8,128)S(1)} %lookup.1), channel_id=1, replica_groups={{320,192,448,64,256,128,384,0},{321,193,449,65,257,129,385,1},{322,194,..., dimensions={0} | all-to-all | bytes 262144 | tf_op jit(solution)/shard_map/all_to_all | solution.py:276
  34.4 10.7 %forces.1 = f32[16,8,256]{2,1,0:T(8,128)} custom-call(s32[4]{0:T(128)S(1)} %pad_add_fusion.where, f32[8,16,256]{2,1,0:T(8,128)S(1)} %all_to_all.10.received, f32[2,15,8192]{2,1,0:T(8,128)S(1)} %all-gather.2.tables), custom_call_target="tpu_custom_call" | custom-call | tf_op jit(solution)/shard_map/forces/pallas_call | solution.py:277
  45.1 0.0 copy-start.1
  45.1 5.5 %all-to-all-start.1 = ((f32[16,8,256]{2,1,0:T(8,128)}), f32[16,8,256]{2,1,0:T(8,128)S(1)}, u32[]{:S(2)}, u32[]{:S(2)}) async-start(f32[16,8,256]{2,1,0:T(8,128)} %forces.1), calls=%async_computation.1 | async-start | bytes 262144 | tf_op jit(solution)/shard_map/all_to_all | solution.py:290
  50.6 0.0 copy-done.1
  50.7 16.5 %all-to-all-done.1.received = f32[16,8,256]{2,1,0:T(8,128)S(1)} async-done(((f32[16,8,256]{2,1,0:T(8,128)}), f32[16,8,256]{2,1,0:T(8,128)S(1)}, u32[]{:S(2)}, u32[]{:S(2)}) %all-to-all-start.1) | async-done | bytes 131104 | tf_op jit(solution)/shard_map/all_to_all | solution.py:290
  67.2 2.1 %all-gather.3 = f32[2,12,512]{2,1,0:T(8,128)S(1)} all-gather(f32[1,12,512]{2,1,0:T(8,128)S(1)} %bitcast.14), channel_id=3, replica_groups=mesh['y'=4,'zh'=2,'core'=2,'xh'=2,'xl'=2,'zl'=8] {'core'}, dimensions={0}, use_global_device_ids=true | all-gather | bytes 73728 | tf_op jit(solution)/shard_map/all_gather | solution.py:299
  69.2 0.6 maximum_select_fusion
  (4 shorter events, 0.0 us)
Async XLA Ops:
  0.0 0.7 copy-start
  0.7 4.6 %copy-start.2 = (f32[12,8192]{1,0:T(8,128)S(1)}, f32[12,8192]{1,0:T(8,128)}, u32[]{:S(2)}) copy-start(f32[12,8192]{1,0:T(8,128)} %state_in.1) | copy-start | bytes 1179652
  0.7 4.6 %copy-start.4 = (s32[8192]{0:T(1024)S(1)}, s32[8192]{0:T(1024)}, u32[]{:S(2)}) copy-start(s32[8192]{0:T(1024)} %param.6) | copy-start | bytes 98308
  0.7 4.6 %copy-start.3 = (f32[8192]{0:T(1024)S(1)}, f32[8192]{0:T(1024)}, u32[]{:S(2)}) copy-start(f32[8192]{0:T(1024)} %param.5) | copy-start | bytes 98308
  0.7 8.5 %collective-permute-start = (s32[8,128]{1,0:T(8,128)S(1)}, s32[8,128]{1,0:T(8,128)S(1)}, u32[]{:S(2)}, u32[]{:S(2)}) collective-permute-start(s32[8,128]{1,0:T(8,128)S(1)} %slots.1.own_slots), channel_id=1, source_target_pairs={{0,24},{8,16},{16,8},{24,0},{1,25},{9,17},{17,9},{25,1},{2,26},{10... | collective-permute-start | bytes 12296 | tf_op jit(solution)/shard_map/ppermute | solution.py:249
  45.1 5.5 %copy-start.1 = (s32[1024]{0:T(1024)S(1)}, s32[1024]{0:T(1024)}, u32[]{:S(2)}) copy-start(s32[1024]{0:T(1024)} %param.7) | copy-start | bytes 12292
  45.1 22.0 %all-to-all-start.1 = ((f32[16,8,256]{2,1,0:T(8,128)}), f32[16,8,256]{2,1,0:T(8,128)S(1)}, u32[]{:S(2)}, u32[]{:S(2)}) async-start(f32[16,8,256]{2,1,0:T(8,128)} %forces.1), calls=%async_computation.1 | async-start | bytes 262144 | tf_op jit(solution)/shard_map/all_to_all | solution.py:290

commit v7 on v6

--- a/solution.py
+++ b/solution.py
@@ -23,8 +23,9 @@
 PART = 256
 SENDERS = 8
 MEMBERS = 16
-NEAR = 8
 Y_ORDER = (2, 1, 3, 0)
+ALONE = [(zh, y, 0) for zh in (1, 0) for y in Y_ORDER]
+PAIRED = [(zh, y, role) for role in (1, 0) for zh in (1, 0) for y in Y_ORDER]
 CHUNK = 512
 UNROLL = 16
 SOURCES = 2 * SHARD
@@ -37,26 +38,21 @@
 dot = functools.partial(lax.dot_general, preferred_element_type=f32)
 
 
-def exchange_groups(columns_of):
-    groups = []
-    for core in range(2):
-        for columns in columns_of:
-            for zl in range(8):
-                groups.append(
-                    [
-                        (((y * 2 + zh) * 2 + core) * 4 + column) * 8 + zl
-                        for zh in ((1, 0) if zl < NEAR else (0, 1))
-                        for y in Y_ORDER
-                        for column in columns
-                    ]
-                )
-    return groups
-
-
-def sender_of(y, zh, zl):
-    near = (zl < NEAR).astype(jnp.int32)
+def exchange_groups(order, columns_of):
+    return [
+        [
+            (((y * 2 + zh) * 2 + core) * 4 + columns[role]) * 8 + zl
+            for zh, y, role in order
+        ]
+        for core in range(2)
+        for columns in columns_of
+        for zl in range(8)
+    ]
+
+
+def sender_of(y, zh):
     place = sum(jnp.where(y == value, k, 0) for k, value in enumerate(Y_ORDER))
-    return jnp.where(zh == near, 0, 4) + place
+    return (1 - zh) * 4 + place
 
 
 def rows_of(value):
@@ -215,11 +211,12 @@
 
 def correct_kernel(received, out):
     for part in range(2):
-        force = received[part]
-        for sender in range(1, SENDERS):
-            force = force + received[2 * sender + part]
-        dt = received[part, 6:7, :]
-        bases = [received[2 * sender + part, 6:7, :] for sender in range(1, 7)]
+        at_member = [PAIRED.index((zh, y, part)) for zh, y, _ in ALONE]
+        force = received[at_member[0]]
+        for member in at_member[1:]:
+            force = force + received[member]
+        dt = received[at_member[0], 6:7, :]
+        bases = [received[member, 6:7, :] for member in at_member[1:7]]
         accel, jerk = force[0:3], force[3:6]
         half = 0.5 * dt
         step_sq = dt * dt * ONE_TWELFTH
@@ -235,7 +232,7 @@
 def local(star_state, star_mass, star_level, active_slots):
     core, helper = lax.axis_index("core"), lax.axis_index("xh")
     y, zh = lax.axis_index("y"), lax.axis_index("zh")
-    sender = sender_of(y, zh, lax.axis_index("zl"))
+    sender = sender_of(y, zh)
     where = jnp.stack([(y * 2 + zh) * SOURCES, core, helper, sender]).astype(jnp.int32)
     slots = pl.pallas_call(
         slots_kernel,
@@ -272,7 +269,7 @@
         compiler_params=PARAMS,
         name="lookup",
     )(where, slots, passed, tables)
-    alone = exchange_groups([(x,) for x in range(4)])
+    alone = exchange_groups(ALONE, [(x,) for x in range(4)])
     received = lax.all_to_all(sent, AXES, 0, 0, axis_index_groups=alone)
     partial = pl.pallas_call(
         force_kernel,
@@ -286,7 +283,7 @@
         compiler_params=PARAMS,
         name="forces",
     )(where, received, tables)
-    paired = exchange_groups([(x, 3 - x) for x in range(2)])
+    paired = exchange_groups(PAIRED, [(x, 3 - x) for x in range(2)])
     shares = lax.all_to_all(partial, AXES, 0, 0, axis_index_groups=paired)
     half_result = pl.pallas_call(
         correct_kernel,

time: 70.2 us -> 69 us (0.983)
  waiting for transfers between devices: 16.5 us -> 14.2 us
  starting transfers between devices: 10 us -> 11 us
    all_to_all x1, waiting for transfers between devices: 16.5 us -> 14.2 us  [local(): shares = lax.all_to_all(partial, AXES, 0, 0, axis_index_groups=paired)]
    all_to_all x1, starting transfers between devices: 5.5 us -> 6.5 us  [local(): shares = lax.all_to_all(partial, AXES, 0, 0, axis_index_groups=paired)]
where the time goes in v7:
time: 69 us; the launch traced here: 68.7 us
  blocking collectives  29.2 us (42%)
  waiting for transfers between devices  14.2 us (21%)
  Pallas kernels  12.8 us (19%)
  starting transfers between devices  11 us (16%)
  other arithmetic  0.72 us (1%)
  local copies, waits for them, and re-layouts  0.71 us (1%)
    all_to_all x1, blocking collectives, local(): received = lax.all_to_all(sent, AXES, 0, 0, axis_index_groups=alone)  23.9 us
    all_to_all x1, waiting for transfers between devices, local(): shares = lax.all_to_all(partial, AXES, 0, 0, axis_index_groups=paired)  14.2 us
    pallas_call x1, Pallas kernels, local(): pl.pallas_call(force_kernel, out_shape=jax.ShapeDtypeStruct((MEMBERS, 8,...  10.7 us
    all_to_all x1, starting transfers between devices, local(): shares = lax.all_to_all(partial, AXES, 0, 0, axis_index_groups=paired)  6.5 us
    ppermute x1, starting transfers between devices, local(): passed = lax.ppermute(slots, ('xh', 'xl'), [(x, 3 - x) for x in range(4)])  4.52 us
    all_gather x1, blocking collectives, local(): tables = lax.all_gather(table, 'core')  3.14 us
    all_gather x1, blocking collectives, local(): halves = lax.all_gather(half_result, 'core')  2.17 us
  transfers between devices with their start and end apart: 2, of which 1 were waited for; matrix products, arithmetic and copies ran while one was open for 0% of the time, Pallas kernels for 1%

profile of v7, /device:TPU:449, one launch (start us, length us, event | category | flops | bytes accessed | tf_op | source)
XLA Modules:
  0.0 68.7 jit_solution(12716664716593602408)
XLA Ops:
  0.0 0.0 copy-start
  0.0 0.7 copy-done
  0.7 0.0 copy-start.2
  0.7 0.0 copy-start.4
  0.7 0.0 copy-start.3
  0.7 4.5 %collective-permute-start = (s32[8,128]{1,0:T(8,128)S(1)}, s32[8,128]{1,0:T(8,128)S(1)}, u32[]{:S(2)}, u32[]{:S(2)}) collective-permute-start(s32[8,128]{1,0:T(8,128)S(1)} %slots.1.own_slots), channel_id=1, source_target_pairs={{0,24},{8,16},{16,8},{24,0},{1,25},{9,17},{17,9},{25,1},{2,26},{10... | collective-permute-start | bytes 12296 | tf_op jit(solution)/shard_map/ppermute | solution.py:246
  5.2 0.0 copy-done.2
  5.3 0.0 copy-done.4
  5.3 0.0 copy-done.3
  5.3 0.7 table.1
  6.0 3.1 %all-gather.2.tables = f32[2,15,8192]{2,1,0:T(8,128)S(1)} all-gather(f32[1,15,8192]{2,1,0:T(8,128)S(1)} %bitcast.13), channel_id=2, replica_groups=mesh['y'=4,'zh'=2,'core'=2,'xh'=2,'xl'=2,'zl'=8] {'core'}, dimensions={0}, use_global_device_ids=true | all-gather | bytes 1474560 | tf_op jit(solution)/shard_map/all_gather | solution.py:263
  9.1 0.1 pad_add_fusion.where
  9.2 0.0 collective-permute-done.passed_slots
  9.2 1.3 %lookup.1 = f32[8,16,256]{2,1,0:T(8,128)S(1)} custom-call(s32[4]{0:T(128)S(1)} %pad_add_fusion.where, s32[8,128]{1,0:T(8,128)S(1)} %slots.1.own_slots, s32[8,128]{1,0:T(8,128)S(1)} %collective-permute-done.passed_slots, f32[2,15,8192]{2,1,0:T(8,128)S(1)} %all-gather.2.tables), custom_call_target="tpu_custom_call" | custom-call | tf_op jit(solution)/shard_map/lookup/pallas_call | solution.py:264
  10.5 23.9 %all_to_all.10.received = f32[8,16,256]{2,1,0:T(8,128)S(1)} all-to-all(f32[8,16,256]{2,1,0:T(8,128)S(1)} %lookup.1), channel_id=1, replica_groups={{320,192,448,64,256,128,384,0},{321,193,449,65,257,129,385,1},{322,194,..., dimensions={0} | all-to-all | bytes 262144 | tf_op jit(solution)/shard_map/all_to_all | solution.py:273
  34.4 10.7 %forces.1 = f32[16,8,256]{2,1,0:T(8,128)} custom-call(s32[4]{0:T(128)S(1)} %pad_add_fusion.where, f32[8,16,256]{2,1,0:T(8,128)S(1)} %all_to_all.10.received, f32[2,15,8192]{2,1,0:T(8,128)S(1)} %all-gather.2.tables), custom_call_target="tpu_custom_call" | custom-call | tf_op jit(solution)/shard_map/forces/pallas_call | solution.py:274
  45.1 0.0 copy-start.1
  45.1 6.5 %all-to-all-start.1 = ((f32[16,8,256]{2,1,0:T(8,128)}), f32[16,8,256]{2,1,0:T(8,128)S(1)}, u32[]{:S(2)}, u32[]{:S(2)}) async-start(f32[16,8,256]{2,1,0:T(8,128)} %forces.1), calls=%async_computation.1 | async-start | bytes 262144 | tf_op jit(solution)/shard_map/all_to_all | solution.py:287
  51.6 0.0 copy-done.1
  51.7 14.2 %all-to-all-done.1.received = f32[16,8,256]{2,1,0:T(8,128)S(1)} async-done(((f32[16,8,256]{2,1,0:T(8,128)}), f32[16,8,256]{2,1,0:T(8,128)S(1)}, u32[]{:S(2)}, u32[]{:S(2)}) %all-to-all-start.1) | async-done | bytes 131104 | tf_op jit(solution)/shard_map/all_to_all | solution.py:287
  65.9 2.2 %all-gather.3 = f32[2,12,512]{2,1,0:T(8,128)S(1)} all-gather(f32[1,12,512]{2,1,0:T(8,128)S(1)} %bitcast.14), channel_id=3, replica_groups=mesh['y'=4,'zh'=2,'core'=2,'xh'=2,'xl'=2,'zl'=8] {'core'}, dimensions={0}, use_global_device_ids=true | all-gather | bytes 73728 | tf_op jit(solution)/shard_map/all_gather | solution.py:296
  68.1 0.6 maximum_select_fusion
  (4 shorter events, 0.0 us)
Async XLA Ops:
  0.0 0.7 copy-start
  0.7 4.6 %copy-start.2 = (f32[12,8192]{1,0:T(8,128)S(1)}, f32[12,8192]{1,0:T(8,128)}, u32[]{:S(2)}) copy-start(f32[12,8192]{1,0:T(8,128)} %state_in.1) | copy-start | bytes 1179652
  0.7 4.6 %copy-start.4 = (s32[8192]{0:T(1024)S(1)}, s32[8192]{0:T(1024)}, u32[]{:S(2)}) copy-start(s32[8192]{0:T(1024)} %param.6) | copy-start | bytes 98308
  0.7 4.6 %copy-start.3 = (f32[8192]{0:T(1024)S(1)}, f32[8192]{0:T(1024)}, u32[]{:S(2)}) copy-start(f32[8192]{0:T(1024)} %param.5) | copy-start | bytes 98308
  0.7 8.5 %collective-permute-start = (s32[8,128]{1,0:T(8,128)S(1)}, s32[8,128]{1,0:T(8,128)S(1)}, u32[]{:S(2)}, u32[]{:S(2)}) collective-permute-start(s32[8,128]{1,0:T(8,128)S(1)} %slots.1.own_slots), channel_id=1, source_target_pairs={{0,24},{8,16},{16,8},{24,0},{1,25},{9,17},{17,9},{25,1},{2,26},{10... | collective-permute-start | bytes 12296 | tf_op jit(solution)/shard_map/ppermute | solution.py:246
  45.1 6.5 %copy-start.1 = (s32[1024]{0:T(1024)S(1)}, s32[1024]{0:T(1024)}, u32[]{:S(2)}) copy-start(s32[1024]{0:T(1024)} %param.7) | copy-start | bytes 12292
  45.1 20.8 %all-to-all-start.1 = ((f32[16,8,256]{2,1,0:T(8,128)}), f32[16,8,256]{2,1,0:T(8,128)S(1)}, u32[]{:S(2)}, u32[]{:S(2)}) async-start(f32[16,8,256]{2,1,0:T(8,128)} %forces.1), calls=%async_computation.1 | async-start | bytes 262144 | tf_op jit(solution)/shard_map/all_to_all | solution.py:287

commit v8 on v7

--- a/solution.py
+++ b/solution.py
@@ -50,11 +50,6 @@
     ]
 
 
-def sender_of(y, zh):
-    place = sum(jnp.where(y == value, k, 0) for k, value in enumerate(Y_ORDER))
-    return (1 - zh) * 4 + place
-
-
 def rows_of(value):
     return lax.broadcasted_iota(jnp.int32, value.shape, 0)
 
@@ -64,6 +59,17 @@
     rest = value - high
     middle = rest.astype(bf16).astype(f32)
     return high, middle, rest - middle
+
+
+def swap_blocks(value):
+    row = rows_of(value)
+    block = lax.broadcasted_iota(jnp.int32, value.shape, 1) >> 5
+    result = jnp.zeros_like(value)
+    for shift in range(8):
+        moved = pltpu.roll(value, 32 * shift, 1) if shift else value
+        kept = jnp.where(block == row, moved, 0.0)
+        result = result + (pltpu.roll(kept, 8 - shift, 0) if shift else kept)
+    return result
 
 
 def high_low(value):
@@ -124,8 +130,11 @@
             found = dot(jnp.concatenate(parts, 1), hits, NN)
             for i in range(16):
                 picked = jnp.where(high == block * 16 + i, found[16 * i : 16 * i + 16], picked)
+    bases = swap_blocks(jnp.where(rows_of(picked[8:16]) < 6, picked[8:16], 0.0))
     for member in range(SENDERS):
-        out[member] = picked
+        out[member, 0:6, :] = picked[0:6]
+        out[member, 6:7, :] = picked[7:8]
+        out[member, 7:8, :] = bases[member : member + 1]
 
 
 def source_features(upper, place_sq):
@@ -170,12 +179,10 @@
     return result
 
 
-def force_kernel(where, received, tables, out, total, rows):
-    target_rows = received[0]
+def force_kernel(received, tables, out, total):
+    target = received[0]
     for sender in range(1, SENDERS):
-        target_rows = target_rows + received[sender]
-    target = target_rows[0:8]
-    rows[...] = target_rows
+        target = target + received[sender]
     radius_part, near_part = target_features(target)
     total[...] = jnp.zeros_like(total)
     for k in range(2):
@@ -201,12 +208,11 @@
     place, speed = target[0:3], target[3:6]
     accel = sums[0:3] - place * sums[6:7]
     jerk = sums[3:6] - speed * sums[6:7] + place * sums[7:8]
-    spare = rows[pl.ds(7 + where[3], 1), :]
     for member in range(MEMBERS):
         out[member, 0:3, :] = accel
         out[member, 3:6, :] = jerk
-        out[member, 6:7, :] = spare
-        out[member, 7:8, :] = spare
+        out[member, 6:7, :] = target[7:8]
+        out[member, 7:8, :] = target[6:7]
 
 
 def correct_kernel(received, out):
@@ -215,13 +221,14 @@
         force = received[at_member[0]]
         for member in at_member[1:]:
             force = force + received[member]
-        dt = received[at_member[0], 6:7, :]
-        bases = [received[member, 6:7, :] for member in at_member[1:7]]
+        dt = received[at_member[0], 7:8, :]
+        pieces = [received[member, 6:7, :] for member in at_member]
+        bases = swap_blocks(jnp.concatenate(pieces, 0))
         accel, jerk = force[0:3], force[3:6]
         half = 0.5 * dt
         step_sq = dt * dt * ONE_TWELFTH
-        velocity = jnp.concatenate(bases[3:6], 0) + half * accel - step_sq * jerk
-        position = jnp.concatenate(bases[0:3], 0) + half * velocity - step_sq * accel
+        velocity = bases[3:6] + half * accel - step_sq * jerk
+        position = bases[0:3] + half * velocity - step_sq * accel
         at = slice(part * PART, (part + 1) * PART)
         out[0:3, at] = position
         out[3:6, at] = velocity
@@ -232,8 +239,7 @@
 def local(star_state, star_mass, star_level, active_slots):
     core, helper = lax.axis_index("core"), lax.axis_index("xh")
     y, zh = lax.axis_index("y"), lax.axis_index("zh")
-    sender = sender_of(y, zh)
-    where = jnp.stack([(y * 2 + zh) * SOURCES, core, helper, sender]).astype(jnp.int32)
+    where = jnp.stack([(y * 2 + zh) * SOURCES, core, helper]).astype(jnp.int32)
     slots = pl.pallas_call(
         slots_kernel,
         out_shape=jax.ShapeDtypeStruct((8, 128), jnp.int32),
@@ -263,7 +269,7 @@
     tables = lax.all_gather(table, "core")
     sent = pl.pallas_call(
         lookup_kernel,
-        out_shape=jax.ShapeDtypeStruct((SENDERS, 16, PART), f32),
+        out_shape=jax.ShapeDtypeStruct((SENDERS, 8, PART), f32),
         in_specs=[SCALARS] + [FULL] * 3,
         out_specs=FULL,
         compiler_params=PARAMS,
@@ -274,15 +280,12 @@
     partial = pl.pallas_call(
         force_kernel,
         out_shape=jax.ShapeDtypeStruct((MEMBERS, 8, PART), f32),
-        in_specs=[SCALARS] + [FULL] * 2,
-        out_specs=FULL,
-        scratch_shapes=[
-            pltpu.VMEM((32, PART), f32),
-            pltpu.VMEM((16, PART), f32),
-        ],
+        in_specs=[FULL] * 2,
+        out_specs=FULL,
+        scratch_shapes=[pltpu.VMEM((32, PART), f32)],
         compiler_params=PARAMS,
         name="forces",
-    )(where, received, tables)
+    )(received, tables)
     paired = exchange_groups(PAIRED, [(x, 3 - x) for x in range(2)])
     shares = lax.all_to_all(partial, AXES, 0, 0, axis_index_groups=paired)
     half_result = pl.pallas_call(

time: 69 us -> 66.8 us (0.968)
  blocking collectives: 29.2 us -> 25.7 us
  waiting for transfers between devices: 14.2 us -> 15.9 us
    all_to_all x1, blocking collectives: 23.9 us -> 20.3 us  [local(): received = lax.all_to_all(sent, AXES, 0, 0, axis_index_groups=alone)]
    all_to_all x1, waiting for transfers between devices: 14.2 us -> 15.9 us  [local(): shares = lax.all_to_all(partial, AXES, 0, 0, axis_index_groups=paired)]
where the time goes in v8:
time: 66.8 us; the launch traced here: 66.5 us
  blocking collectives  25.7 us (38%)
  waiting for transfers between devices  15.9 us (24%)
  Pallas kernels  12.4 us (19%)
  starting transfers between devices  11 us (16%)
  other arithmetic  0.72 us (1%)
  local copies, waits for them, and re-layouts  0.71 us (1%)
    all_to_all x1, blocking collectives, local(): received = lax.all_to_all(sent, AXES, 0, 0, axis_index_groups=alone)  20.3 us
    all_to_all x1, waiting for transfers between devices, local(): shares = lax.all_to_all(partial, AXES, 0, 0, axis_index_groups=paired)  15.9 us
    pallas_call x1, Pallas kernels, local(): pl.pallas_call(force_kernel, out_shape=jax.ShapeDtypeStruct((MEMBERS, 8,...  10.2 us
    all_to_all x1, starting transfers between devices, local(): shares = lax.all_to_all(partial, AXES, 0, 0, axis_index_groups=paired)  6.5 us
    ppermute x1, starting transfers between devices, local(): passed = lax.ppermute(slots, ('xh', 'xl'), [(x, 3 - x) for x in range(4)])  4.52 us
    all_gather x1, blocking collectives, local(): tables = lax.all_gather(table, 'core')  3.14 us
    all_gather x1, blocking collectives, local(): halves = lax.all_gather(half_result, 'core')  2.23 us
    pallas_call x1, Pallas kernels, local(): pl.pallas_call(lookup_kernel, out_shape=jax.ShapeDtypeStruct((SENDERS, 8,...  1.39 us
  transfers between devices with their start and end apart: 2, of which 1 were waited for; matrix products, arithmetic and copies ran while one was open for 0% of the time, Pallas kernels for 1%

profile of v8, /device:TPU:449, one launch (start us, length us, event | category | flops | bytes accessed | tf_op | source)
XLA Modules:
  0.0 66.5 jit_solution(9964668993008272642)
XLA Ops:
  0.0 0.0 copy-start
  0.0 0.7 %copy-done = s32[1024]{0:T(1024)S(1)} copy-done((s32[1024]{0:T(1024)S(1)}, s32[1024]{0:T(1024)}, u32[]{:S(2)}) %copy-start) | copy-done | bytes 4120
  0.7 0.0 copy-start.2
  0.7 0.0 copy-start.3
  0.7 0.0 copy-start.4
  0.7 4.5 %collective-permute-start = (s32[8,128]{1,0:T(8,128)S(1)}, s32[8,128]{1,0:T(8,128)S(1)}, u32[]{:S(2)}, u32[]{:S(2)}) collective-permute-start(s32[8,128]{1,0:T(8,128)S(1)} %slots.1.own_slots), channel_id=1, source_target_pairs={{0,24},{8,16},{16,8},{24,0},{1,25},{9,17},{17,9},{25,1},{2,26},{10... | collective-permute-start | bytes 12296 | tf_op jit(solution)/shard_map/ppermute | solution.py:252
  5.2 0.0 copy-done.2
  5.2 0.0 copy-done.3
  5.3 0.0 copy-done.4
  5.3 0.7 %table.1 = f32[15,8192]{1,0:T(8,128)S(1)} custom-call(f32[12,8192]{1,0:T(8,128)S(1)} %copy-done.2, f32[1,8192]{1,0:T(1,128)S(1)} %bitcast.15, s32[1,8192]{1,0:T(1,128)S(1)} %bitcast.16), custom_call_target="tpu_custom_call" | custom-call | flops 10000000000 | bytes 16777216 | tf_op jit(solution)/shard_map/table/pallas_call | solution.py:254
  5.9 3.1 %all-gather.2.tables = f32[2,15,8192]{2,1,0:T(8,128)S(1)} all-gather(f32[1,15,8192]{2,1,0:T(8,128)S(1)} %bitcast.12), channel_id=2, replica_groups=mesh['y'=4,'zh'=2,'core'=2,'xh'=2,'xl'=2,'zl'=8] {'core'}, dimensions={0}, use_global_device_ids=true | all-gather | bytes 1474560 | tf_op jit(solution)/shard_map/all_gather | solution.py:269
  9.1 0.1 pad_add_fusion.where
  9.2 0.0 collective-permute-done.passed_slots
  9.2 1.4 %lookup.1 = f32[8,8,256]{2,1,0:T(8,128)S(1)} custom-call(s32[3]{0:T(128)S(1)} %pad_add_fusion.where, s32[8,128]{1,0:T(8,128)S(1)} %slots.1.own_slots, s32[8,128]{1,0:T(8,128)S(1)} %collective-permute-done.passed_slots, f32[2,15,8192]{2,1,0:T(8,128)S(1)} %all-gather.2.tables), custom_call_target="tpu_custom_call" | custom-call | tf_op jit(solution)/shard_map/lookup/pallas_call | solution.py:270
  10.6 20.3 %all_to_all.10.received = f32[8,8,256]{2,1,0:T(8,128)S(1)} all-to-all(f32[8,8,256]{2,1,0:T(8,128)S(1)} %lookup.1), channel_id=1, replica_groups={{320,192,448,64,256,128,384,0},{321,193,449,65,257,129,385,1},{322,194,..., dimensions={0} | all-to-all | bytes 131072 | tf_op jit(solution)/shard_map/all_to_all | solution.py:279
  30.9 10.2 %forces.1 = f32[16,8,256]{2,1,0:T(8,128)} custom-call(f32[8,8,256]{2,1,0:T(8,128)S(1)} %all_to_all.10.received, f32[2,15,8192]{2,1,0:T(8,128)S(1)} %all-gather.2.tables), custom_call_target="tpu_custom_call" | custom-call | tf_op jit(solution)/shard_map/forces/pallas_call | solution.py:280
  41.1 0.0 copy-start.1
  41.1 6.5 %all-to-all-start.1 = ((f32[16,8,256]{2,1,0:T(8,128)}), f32[16,8,256]{2,1,0:T(8,128)S(1)}, u32[]{:S(2)}, u32[]{:S(2)}) async-start(f32[16,8,256]{2,1,0:T(8,128)} %forces.1), calls=%async_computation.1 | async-start | bytes 262144 | tf_op jit(solution)/shard_map/all_to_all | solution.py:290
  47.6 0.0 copy-done.1
  47.6 15.9 %all-to-all-done.1.received = f32[16,8,256]{2,1,0:T(8,128)S(1)} async-done(((f32[16,8,256]{2,1,0:T(8,128)}), f32[16,8,256]{2,1,0:T(8,128)S(1)}, u32[]{:S(2)}, u32[]{:S(2)}) %all-to-all-start.1) | async-done | bytes 131104 | tf_op jit(solution)/shard_map/all_to_all | solution.py:290
  63.5 0.1 corrector.1
  63.6 2.2 %all-gather.3 = f32[2,12,512]{2,1,0:T(8,128)S(1)} all-gather(f32[1,12,512]{2,1,0:T(8,128)S(1)} %bitcast.13), channel_id=3, replica_groups=mesh['y'=4,'zh'=2,'core'=2,'xh'=2,'xl'=2,'zl'=8] {'core'}, dimensions={0}, use_global_device_ids=true | all-gather | bytes 73728 | tf_op jit(solution)/shard_map/all_gather | solution.py:299
  65.9 0.6 maximum_select_fusion
  (3 shorter events, 0.0 us)
Async XLA Ops:
  0.0 0.7 %copy-start = (s32[1024]{0:T(1024)S(1)}, s32[1024]{0:T(1024)}, u32[]{:S(2)}) copy-start(s32[1024]{0:T(1024)} %param.7) | copy-start | bytes 12292
  0.7 4.5 %copy-start.2 = (f32[12,8192]{1,0:T(8,128)S(1)}, f32[12,8192]{1,0:T(8,128)}, u32[]{:S(2)}) copy-start(f32[12,8192]{1,0:T(8,128)} %state_in.1) | copy-start | bytes 1179652
  0.7 4.6 %copy-start.3 = (f32[8192]{0:T(1024)S(1)}, f32[8192]{0:T(1024)}, u32[]{:S(2)}) copy-start(f32[8192]{0:T(1024)} %param.5) | copy-start | bytes 98308
  0.7 4.6 %copy-start.4 = (s32[8192]{0:T(1024)S(1)}, s32[8192]{0:T(1024)}, u32[]{:S(2)}) copy-start(s32[8192]{0:T(1024)} %param.6) | copy-start | bytes 98308
  0.7 8.5 %collective-permute-start = (s32[8,128]{1,0:T(8,128)S(1)}, s32[8,128]{1,0:T(8,128)S(1)}, u32[]{:S(2)}, u32[]{:S(2)}) collective-permute-start(s32[8,128]{1,0:T(8,128)S(1)} %slots.1.own_slots), channel_id=1, source_target_pairs={{0,24},{8,16},{16,8},{24,0},{1,25},{9,17},{17,9},{25,1},{2,26},{10... | collective-permute-start | bytes 12296 | tf_op jit(solution)/shard_map/ppermute | solution.py:252
  41.1 6.5 %copy-start.1 = (s32[1024]{0:T(1024)S(1)}, s32[1024]{0:T(1024)}, u32[]{:S(2)}) copy-start(s32[1024]{0:T(1024)} %param.7) | copy-start | bytes 12292
  41.1 22.4 %all-to-all-start.1 = ((f32[16,8,256]{2,1,0:T(8,128)}), f32[16,8,256]{2,1,0:T(8,128)S(1)}, u32[]{:S(2)}, u32[]{:S(2)}) async-start(f32[16,8,256]{2,1,0:T(8,128)} %forces.1), calls=%async_computation.1 | async-start | bytes 262144 | tf_op jit(solution)/shard_map/all_to_all | solution.py:290

commit v9 on v8

--- a/solution.py
+++ b/solution.py
@@ -18,7 +18,7 @@
 BLK = ("y", "zh", "core")
 ACT = ("xh", "xl", "zl")
 SHARD = 8192
-ROWS = 15
+ROWS = 14
 HALF = 512
 PART = 256
 SENDERS = 8
@@ -105,7 +105,6 @@
     table[7:8, :] = dt
     table[8:11, :] = x + half * v + step_sq * a
     table[11:14, :] = v + half * a + step_sq * j
-    table[14:15, :] = jnp.sum(place * place, 0, keepdims=True)
 
 
 def lookup_kernel(where, own_slots, passed_slots, tables, out):
@@ -137,8 +136,9 @@
         out[member, 7:8, :] = bases[member : member + 1]
 
 
-def source_features(upper, place_sq):
+def source_features(upper):
     row = rows_of(upper)
+    place_sq = jnp.sum(jnp.where(row < 3, upper * upper, 0.0), 0, keepdims=True)
     speed = pltpu.roll(upper, 5, 0)
     product = 3.0 * jnp.sum(jnp.where(row < 3, upper * speed, 0.0), 0, keepdims=True)
     a, b, c = split(jnp.where(row == 7, 1.0, upper))
@@ -183,13 +183,16 @@
     target = received[0]
     for sender in range(1, SENDERS):
         target = target + received[sender]
+    centre = sum(jnp.sum(tables[k, 0:8, :], 1, keepdims=True) for k in range(2))
+    centre = jnp.where(rows_of(centre) < 6, centre * (1.0 / SOURCES), 0.0)
+    target = target - centre
     radius_part, near_part = target_features(target)
     total[...] = jnp.zeros_like(total)
     for k in range(2):
 
         def step(turn, _, k=k):
             at = pl.ds(pl.multiple_of(turn * CHUNK, CHUNK), CHUNK)
-            source, pull, swing = source_features(tables[k, 0:8, at], tables[k, 14:15, at])
+            source, pull, swing = source_features(tables[k, 0:8, at] - centre)
             radius_sq = dot(source, radius_part, TN)
             product = dot(source, near_part, TN)
             inverse = lax.rsqrt(radius_sq)

time: 66.8 us -> 68.1 us (1.019)
  Pallas kernels: 12.4 us -> 13.6 us
    pallas_call x1, Pallas kernels: 10.2 us -> 11.5 us  [local(): pl.pallas_call(force_kernel, out_shape=jax.ShapeDtypeStruct((MEMBERS, 8,...]
where the time goes in v9:
time: 68.1 us; the launch traced here: 67.8 us
  blocking collectives  25.7 us (38%)
  waiting for transfers between devices  15.9 us (23%)
  Pallas kernels  13.6 us (20%)
  starting transfers between devices  11 us (16%)
  other arithmetic  0.72 us (1%)
  local copies, waits for them, and re-layouts  0.71 us (1%)
    all_to_all x1, blocking collectives, local(): received = lax.all_to_all(sent, AXES, 0, 0, axis_index_groups=alone)  20.4 us
    all_to_all x1, waiting for transfers between devices, local(): shares = lax.all_to_all(partial, AXES, 0, 0, axis_index_groups=paired)  15.9 us
    pallas_call x1, Pallas kernels, local(): pl.pallas_call(force_kernel, out_shape=jax.ShapeDtypeStruct((MEMBERS, 8,...  11.5 us
    all_to_all x1, starting transfers between devices, local(): shares = lax.all_to_all(partial, AXES, 0, 0, axis_index_groups=paired)  6.5 us
    ppermute x1, starting transfers between devices, local(): passed = lax.ppermute(slots, ('xh', 'xl'), [(x, 3 - x) for x in range(4)])  4.52 us
    all_gather x1, blocking collectives, local(): tables = lax.all_gather(table, 'core')  3.14 us
    all_gather x1, blocking collectives, local(): halves = lax.all_gather(half_result, 'core')  2.24 us
    pallas_call x1, Pallas kernels, local(): pl.pallas_call(lookup_kernel, out_shape=jax.ShapeDtypeStruct((SENDERS, 8,...  1.39 us
  transfers between devices with their start and end apart: 2, of which 1 were waited for; matrix products, arithmetic and copies ran while one was open for 0% of the time, Pallas kernels for 1%

profile of v9, /device:TPU:449, one launch (start us, length us, event | category | flops | bytes accessed | tf_op | source)
XLA Modules:
  0.0 67.8 jit_solution(15842425125789021028)
XLA Ops:
  0.0 0.0 copy-start
  0.0 0.7 %copy-done = s32[1024]{0:T(1024)S(1)} copy-done((s32[1024]{0:T(1024)S(1)}, s32[1024]{0:T(1024)}, u32[]{:S(2)}) %copy-start) | copy-done | bytes 4120
  0.7 0.0 copy-start.2
  0.7 0.0 copy-start.3
  0.7 0.0 copy-start.4
  0.7 4.5 %collective-permute-start = (s32[8,128]{1,0:T(8,128)S(1)}, s32[8,128]{1,0:T(8,128)S(1)}, u32[]{:S(2)}, u32[]{:S(2)}) collective-permute-start(s32[8,128]{1,0:T(8,128)S(1)} %slots.1.own_slots), channel_id=1, source_target_pairs={{0,24},{8,16},{16,8},{24,0},{1,25},{9,17},{17,9},{25,1},{2,26},{10... | collective-permute-start | bytes 12296 | tf_op jit(solution)/shard_map/ppermute | solution.py:255
  5.2 0.0 copy-done.2
  5.2 0.0 copy-done.3
  5.3 0.0 copy-done.4
  5.3 0.6 table.1
  5.9 3.1 %all-gather.2.tables = f32[2,14,8192]{2,1,0:T(8,128)S(1)} all-gather(f32[1,14,8192]{2,1,0:T(8,128)S(1)} %bitcast.12), channel_id=2, replica_groups=mesh['y'=4,'zh'=2,'core'=2,'xh'=2,'xl'=2,'zl'=8] {'core'}, dimensions={0}, use_global_device_ids=true | all-gather | bytes 1376256 | tf_op jit(solution)/shard_map/all_gather | solution.py:272
  9.0 0.1 pad_add_fusion.where
  9.1 0.0 collective-permute-done.passed_slots
  9.1 1.4 %lookup.1 = f32[8,8,256]{2,1,0:T(8,128)S(1)} custom-call(s32[3]{0:T(128)S(1)} %pad_add_fusion.where, s32[8,128]{1,0:T(8,128)S(1)} %slots.1.own_slots, s32[8,128]{1,0:T(8,128)S(1)} %collective-permute-done.passed_slots, f32[2,14,8192]{2,1,0:T(8,128)S(1)} %all-gather.2.tables), custom_call_target="tpu_custom_call" | custom-call | tf_op jit(solution)/shard_map/lookup/pallas_call | solution.py:273
  10.5 20.4 %all_to_all.10.received = f32[8,8,256]{2,1,0:T(8,128)S(1)} all-to-all(f32[8,8,256]{2,1,0:T(8,128)S(1)} %lookup.1), channel_id=1, replica_groups={{320,192,448,64,256,128,384,0},{321,193,449,65,257,129,385,1},{322,194,..., dimensions={0} | all-to-all | bytes 131072 | tf_op jit(solution)/shard_map/all_to_all | solution.py:282
  30.8 11.5 %forces.1 = f32[16,8,256]{2,1,0:T(8,128)} custom-call(f32[8,8,256]{2,1,0:T(8,128)S(1)} %all_to_all.10.received, f32[2,14,8192]{2,1,0:T(8,128)S(1)} %all-gather.2.tables), custom_call_target="tpu_custom_call" | custom-call | tf_op jit(solution)/shard_map/forces/pallas_call | solution.py:283
  42.4 0.0 copy-start.1
  42.4 6.5 %all-to-all-start.1 = ((f32[16,8,256]{2,1,0:T(8,128)}), f32[16,8,256]{2,1,0:T(8,128)S(1)}, u32[]{:S(2)}, u32[]{:S(2)}) async-start(f32[16,8,256]{2,1,0:T(8,128)} %forces.1), calls=%async_computation.1 | async-start | bytes 262144 | tf_op jit(solution)/shard_map/all_to_all | solution.py:293
  48.9 0.0 copy-done.1
  48.9 15.9 %all-to-all-done.1.received = f32[16,8,256]{2,1,0:T(8,128)S(1)} async-done(((f32[16,8,256]{2,1,0:T(8,128)}), f32[16,8,256]{2,1,0:T(8,128)S(1)}, u32[]{:S(2)}, u32[]{:S(2)}) %all-to-all-start.1) | async-done | bytes 131104 | tf_op jit(solution)/shard_map/all_to_all | solution.py:293
  64.8 0.1 corrector.1
  64.9 2.2 %all-gather.3 = f32[2,12,512]{2,1,0:T(8,128)S(1)} all-gather(f32[1,12,512]{2,1,0:T(8,128)S(1)} %bitcast.13), channel_id=3, replica_groups=mesh['y'=4,'zh'=2,'core'=2,'xh'=2,'xl'=2,'zl'=8] {'core'}, dimensions={0}, use_global_device_ids=true | all-gather | bytes 73728 | tf_op jit(solution)/shard_map/all_gather | solution.py:302
  67.1 0.6 maximum_select_fusion
  (3 shorter events, 0.0 us)
Async XLA Ops:
  0.0 0.7 %copy-start = (s32[1024]{0:T(1024)S(1)}, s32[1024]{0:T(1024)}, u32[]{:S(2)}) copy-start(s32[1024]{0:T(1024)} %param.7) | copy-start | bytes 12292
  0.7 4.5 %copy-start.2 = (f32[12,8192]{1,0:T(8,128)S(1)}, f32[12,8192]{1,0:T(8,128)}, u32[]{:S(2)}) copy-start(f32[12,8192]{1,0:T(8,128)} %state_in.1) | copy-start | bytes 1179652
  0.7 4.6 %copy-start.3 = (f32[8192]{0:T(1024)S(1)}, f32[8192]{0:T(1024)}, u32[]{:S(2)}) copy-start(f32[8192]{0:T(1024)} %param.5) | copy-start | bytes 98308
  0.7 4.6 %copy-start.4 = (s32[8192]{0:T(1024)S(1)}, s32[8192]{0:T(1024)}, u32[]{:S(2)}) copy-start(s32[8192]{0:T(1024)} %param.6) | copy-start | bytes 98308
  0.7 8.4 %collective-permute-start = (s32[8,128]{1,0:T(8,128)S(1)}, s32[8,128]{1,0:T(8,128)S(1)}, u32[]{:S(2)}, u32[]{:S(2)}) collective-permute-start(s32[8,128]{1,0:T(8,128)S(1)} %slots.1.own_slots), channel_id=1, source_target_pairs={{0,24},{8,16},{16,8},{24,0},{1,25},{9,17},{17,9},{25,1},{2,26},{10... | collective-permute-start | bytes 12296 | tf_op jit(solution)/shard_map/ppermute | solution.py:255
  42.4 6.5 %copy-start.1 = (s32[1024]{0:T(1024)S(1)}, s32[1024]{0:T(1024)}, u32[]{:S(2)}) copy-start(s32[1024]{0:T(1024)} %param.7) | copy-start | bytes 12292
  42.4 22.4 %all-to-all-start.1 = ((f32[16,8,256]{2,1,0:T(8,128)}), f32[16,8,256]{2,1,0:T(8,128)S(1)}, u32[]{:S(2)}, u32[]{:S(2)}) async-start(f32[16,8,256]{2,1,0:T(8,128)} %forces.1), calls=%async_computation.1 | async-start | bytes 262144 | tf_op jit(solution)/shard_map/all_to_all | solution.py:293

commit v10 on v9

--- a/solution.py
+++ b/solution.py
@@ -19,6 +19,7 @@
 ACT = ("xh", "xl", "zl")
 SHARD = 8192
 ROWS = 14
+SAMPLE = 1024
 HALF = 512
 PART = 256
 SENDERS = 8
@@ -183,8 +184,8 @@
     target = received[0]
     for sender in range(1, SENDERS):
         target = target + received[sender]
-    centre = sum(jnp.sum(tables[k, 0:8, :], 1, keepdims=True) for k in range(2))
-    centre = jnp.where(rows_of(centre) < 6, centre * (1.0 / SOURCES), 0.0)
+    centre = jnp.sum(tables[0, 0:8, 0:SAMPLE], 1, keepdims=True)
+    centre = jnp.where(rows_of(centre) < 6, centre * (1.0 / SAMPLE), 0.0)
     target = target - centre
     radius_part, near_part = target_features(target)
     total[...] = jnp.zeros_like(total)

time: 68.1 us -> 68 us (level)
  no operation moved by 1% of the time
where the time goes in v10:
time: 68 us; the launch traced here: 67.7 us
  blocking collectives  25.7 us (38%)
  waiting for transfers between devices  15.9 us (23%)
  Pallas kernels  13.6 us (20%)
  starting transfers between devices  11 us (16%)
  other arithmetic  0.72 us (1%)
  local copies, waits for them, and re-layouts  0.71 us (1%)
    all_to_all x1, blocking collectives, local(): received = lax.all_to_all(sent, AXES, 0, 0, axis_index_groups=alone)  20.4 us
    all_to_all x1, waiting for transfers between devices, local(): shares = lax.all_to_all(partial, AXES, 0, 0, axis_index_groups=paired)  15.9 us
    pallas_call x1, Pallas kernels, local(): pl.pallas_call(force_kernel, out_shape=jax.ShapeDtypeStruct((MEMBERS, 8,...  11.5 us
    all_to_all x1, starting transfers between devices, local(): shares = lax.all_to_all(partial, AXES, 0, 0, axis_index_groups=paired)  6.5 us
    ppermute x1, starting transfers between devices, local(): passed = lax.ppermute(slots, ('xh', 'xl'), [(x, 3 - x) for x in range(4)])  4.52 us
    all_gather x1, blocking collectives, local(): tables = lax.all_gather(table, 'core')  3.14 us
    all_gather x1, blocking collectives, local(): halves = lax.all_gather(half_result, 'core')  2.24 us
    pallas_call x1, Pallas kernels, local(): pl.pallas_call(lookup_kernel, out_shape=jax.ShapeDtypeStruct((SENDERS, 8,...  1.39 us
  transfers between devices with their start and end apart: 2, of which 1 were waited for; matrix products, arithmetic and copies ran while one was open for 0% of the time, Pallas kernels for 1%

profile of v10, /device:TPU:449, one launch (start us, length us, event | category | flops | bytes accessed | tf_op | source)
XLA Modules:
  0.0 67.7 jit_solution(9878322235087742450)
XLA Ops:
  0.0 0.0 copy-start
  0.0 0.7 %copy-done = s32[1024]{0:T(1024)S(1)} copy-done((s32[1024]{0:T(1024)S(1)}, s32[1024]{0:T(1024)}, u32[]{:S(2)}) %copy-start) | copy-done | bytes 4120
  0.7 0.0 copy-start.2
  0.7 0.0 copy-start.3
  0.7 0.0 copy-start.4
  0.7 4.5 %collective-permute-start = (s32[8,128]{1,0:T(8,128)S(1)}, s32[8,128]{1,0:T(8,128)S(1)}, u32[]{:S(2)}, u32[]{:S(2)}) collective-permute-start(s32[8,128]{1,0:T(8,128)S(1)} %slots.1.own_slots), channel_id=1, source_target_pairs={{0,24},{8,16},{16,8},{24,0},{1,25},{9,17},{17,9},{25,1},{2,26},{10... | collective-permute-start | bytes 12296 | tf_op jit(solution)/shard_map/ppermute | solution.py:256
  5.2 0.0 copy-done.2
  5.2 0.0 copy-done.3
  5.3 0.0 copy-done.4
  5.3 0.6 table.1
  5.9 3.1 %all-gather.2.tables = f32[2,14,8192]{2,1,0:T(8,128)S(1)} all-gather(f32[1,14,8192]{2,1,0:T(8,128)S(1)} %bitcast.12), channel_id=2, replica_groups=mesh['y'=4,'zh'=2,'core'=2,'xh'=2,'xl'=2,'zl'=8] {'core'}, dimensions={0}, use_global_device_ids=true | all-gather | bytes 1376256 | tf_op jit(solution)/shard_map/all_gather | solution.py:273
  9.0 0.1 pad_add_fusion.where
  9.1 0.0 collective-permute-done.passed_slots
  9.1 1.4 %lookup.1 = f32[8,8,256]{2,1,0:T(8,128)S(1)} custom-call(s32[3]{0:T(128)S(1)} %pad_add_fusion.where, s32[8,128]{1,0:T(8,128)S(1)} %slots.1.own_slots, s32[8,128]{1,0:T(8,128)S(1)} %collective-permute-done.passed_slots, f32[2,14,8192]{2,1,0:T(8,128)S(1)} %all-gather.2.tables), custom_call_target="tpu_custom_call" | custom-call | tf_op jit(solution)/shard_map/lookup/pallas_call | solution.py:274
  10.5 20.4 %all_to_all.10.received = f32[8,8,256]{2,1,0:T(8,128)S(1)} all-to-all(f32[8,8,256]{2,1,0:T(8,128)S(1)} %lookup.1), channel_id=1, replica_groups={{320,192,448,64,256,128,384,0},{321,193,449,65,257,129,385,1},{322,194,..., dimensions={0} | all-to-all | bytes 131072 | tf_op jit(solution)/shard_map/all_to_all | solution.py:283
  30.8 11.5 %forces.1 = f32[16,8,256]{2,1,0:T(8,128)} custom-call(f32[8,8,256]{2,1,0:T(8,128)S(1)} %all_to_all.10.received, f32[2,14,8192]{2,1,0:T(8,128)S(1)} %all-gather.2.tables), custom_call_target="tpu_custom_call" | custom-call | tf_op jit(solution)/shard_map/forces/pallas_call | solution.py:284
  42.3 0.0 copy-start.1
  42.3 6.5 %all-to-all-start.1 = ((f32[16,8,256]{2,1,0:T(8,128)}), f32[16,8,256]{2,1,0:T(8,128)S(1)}, u32[]{:S(2)}, u32[]{:S(2)}) async-start(f32[16,8,256]{2,1,0:T(8,128)} %forces.1), calls=%async_computation.1 | async-start | bytes 262144 | tf_op jit(solution)/shard_map/all_to_all | solution.py:294
  48.8 0.0 copy-done.1
  48.8 15.9 %all-to-all-done.1.received = f32[16,8,256]{2,1,0:T(8,128)S(1)} async-done(((f32[16,8,256]{2,1,0:T(8,128)}), f32[16,8,256]{2,1,0:T(8,128)S(1)}, u32[]{:S(2)}, u32[]{:S(2)}) %all-to-all-start.1) | async-done | bytes 131104 | tf_op jit(solution)/shard_map/all_to_all | solution.py:294
  64.7 0.1 corrector.1
  64.8 2.2 %all-gather.3 = f32[2,12,512]{2,1,0:T(8,128)S(1)} all-gather(f32[1,12,512]{2,1,0:T(8,128)S(1)} %bitcast.13), channel_id=3, replica_groups=mesh['y'=4,'zh'=2,'core'=2,'xh'=2,'xl'=2,'zl'=8] {'core'}, dimensions={0}, use_global_device_ids=true | all-gather | bytes 73728 | tf_op jit(solution)/shard_map/all_gather | solution.py:303
  67.1 0.6 maximum_select_fusion
  (3 shorter events, 0.0 us)
Async XLA Ops:
  0.0 0.7 %copy-start = (s32[1024]{0:T(1024)S(1)}, s32[1024]{0:T(1024)}, u32[]{:S(2)}) copy-start(s32[1024]{0:T(1024)} %param.7) | copy-start | bytes 12292
  0.7 4.5 %copy-start.2 = (f32[12,8192]{1,0:T(8,128)S(1)}, f32[12,8192]{1,0:T(8,128)}, u32[]{:S(2)}) copy-start(f32[12,8192]{1,0:T(8,128)} %state_in.1) | copy-start | bytes 1179652
  0.7 4.6 %copy-start.3 = (f32[8192]{0:T(1024)S(1)}, f32[8192]{0:T(1024)}, u32[]{:S(2)}) copy-start(f32[8192]{0:T(1024)} %param.5) | copy-start | bytes 98308
  0.7 4.6 %copy-start.4 = (s32[8192]{0:T(1024)S(1)}, s32[8192]{0:T(1024)}, u32[]{:S(2)}) copy-start(s32[8192]{0:T(1024)} %param.6) | copy-start | bytes 98308
  0.7 8.4 %collective-permute-start = (s32[8,128]{1,0:T(8,128)S(1)}, s32[8,128]{1,0:T(8,128)S(1)}, u32[]{:S(2)}, u32[]{:S(2)}) collective-permute-start(s32[8,128]{1,0:T(8,128)S(1)} %slots.1.own_slots), channel_id=1, source_target_pairs={{0,24},{8,16},{16,8},{24,0},{1,25},{9,17},{17,9},{25,1},{2,26},{10... | collective-permute-start | bytes 12296 | tf_op jit(solution)/shard_map/ppermute | solution.py:256
  42.3 6.5 %copy-start.1 = (s32[1024]{0:T(1024)S(1)}, s32[1024]{0:T(1024)}, u32[]{:S(2)}) copy-start(s32[1024]{0:T(1024)} %param.7) | copy-start | bytes 12292
  42.3 22.4 %all-to-all-start.1 = ((f32[16,8,256]{2,1,0:T(8,128)}), f32[16,8,256]{2,1,0:T(8,128)S(1)}, u32[]{:S(2)}, u32[]{:S(2)}) async-start(f32[16,8,256]{2,1,0:T(8,128)} %forces.1), calls=%async_computation.1 | async-start | bytes 262144 | tf_op jit(solution)/shard_map/all_to_all | solution.py:294

commit v11 on v10

--- a/solution.py
+++ b/solution.py
@@ -19,7 +19,7 @@
 ACT = ("xh", "xl", "zl")
 SHARD = 8192
 ROWS = 14
-SAMPLE = 1024
+SAMPLE = 128
 HALF = 512
 PART = 256
 SENDERS = 8
@@ -27,8 +27,8 @@
 Y_ORDER = (2, 1, 3, 0)
 ALONE = [(zh, y, 0) for zh in (1, 0) for y in Y_ORDER]
 PAIRED = [(zh, y, role) for role in (1, 0) for zh in (1, 0) for y in Y_ORDER]
-CHUNK = 512
-UNROLL = 16
+CHUNK = 256
+UNROLL = 32
 SOURCES = 2 * SHARD
 FULL = pl.BlockSpec(memory_space=pltpu.VMEM)
 SCALARS = pl.BlockSpec(memory_space=pltpu.SMEM)

time: 68 us -> 67.1 us (0.987)
  Pallas kernels: 13.6 us -> 12.7 us
    pallas_call x1, Pallas kernels: 11.5 us -> 10.6 us  [local(): pl.pallas_call(force_kernel, out_shape=jax.ShapeDtypeStruct((MEMBERS, 8,...]
where the time goes in v11:
time: 67.1 us; the launch traced here: 66.8 us
  blocking collectives  25.7 us (38%)
  waiting for transfers between devices  15.9 us (24%)
  Pallas kernels  12.7 us (19%)
  starting transfers between devices  11 us (16%)
  other arithmetic  0.72 us (1%)
  local copies, waits for them, and re-layouts  0.71 us (1%)
    all_to_all x1, blocking collectives, local(): received = lax.all_to_all(sent, AXES, 0, 0, axis_index_groups=alone)  20.4 us
    all_to_all x1, waiting for transfers between devices, local(): shares = lax.all_to_all(partial, AXES, 0, 0, axis_index_groups=paired)  15.9 us
    pallas_call x1, Pallas kernels, local(): pl.pallas_call(force_kernel, out_shape=jax.ShapeDtypeStruct((MEMBERS, 8,...  10.6 us
    all_to_all x1, starting transfers between devices, local(): shares = lax.all_to_all(partial, AXES, 0, 0, axis_index_groups=paired)  6.5 us
    ppermute x1, starting transfers between devices, local(): passed = lax.ppermute(slots, ('xh', 'xl'), [(x, 3 - x) for x in range(4)])  4.52 us
    all_gather x1, blocking collectives, local(): tables = lax.all_gather(table, 'core')  3.14 us
    all_gather x1, blocking collectives, local(): halves = lax.all_gather(half_result, 'core')  2.24 us
    pallas_call x1, Pallas kernels, local(): pl.pallas_call(lookup_kernel, out_shape=jax.ShapeDtypeStruct((SENDERS, 8,...  1.39 us
  transfers between devices with their start and end apart: 2, of which 1 were waited for; matrix products, arithmetic and copies ran while one was open for 0% of the time, Pallas kernels for 1%

profile of v11, /device:TPU:449, one launch (start us, length us, event | category | flops | bytes accessed | tf_op | source)
XLA Modules:
  0.0 66.8 jit_solution(11256048477862101439)
XLA Ops:
  0.0 0.0 copy-start
  0.0 0.7 %copy-done = s32[1024]{0:T(1024)S(1)} copy-done((s32[1024]{0:T(1024)S(1)}, s32[1024]{0:T(1024)}, u32[]{:S(2)}) %copy-start) | copy-done | bytes 4120
  0.7 0.0 copy-start.2
  0.7 0.0 copy-start.3
  0.7 0.0 copy-start.4
  0.7 4.5 %collective-permute-start = (s32[8,128]{1,0:T(8,128)S(1)}, s32[8,128]{1,0:T(8,128)S(1)}, u32[]{:S(2)}, u32[]{:S(2)}) collective-permute-start(s32[8,128]{1,0:T(8,128)S(1)} %slots.1.own_slots), channel_id=1, source_target_pairs={{0,24},{8,16},{16,8},{24,0},{1,25},{9,17},{17,9},{25,1},{2,26},{10... | collective-permute-start | bytes 12296 | tf_op jit(solution)/shard_map/ppermute | solution.py:256
  5.2 0.0 copy-done.2
  5.2 0.0 copy-done.3
  5.3 0.0 copy-done.4
  5.3 0.6 table.1
  5.9 3.1 %all-gather.2.tables = f32[2,14,8192]{2,1,0:T(8,128)S(1)} all-gather(f32[1,14,8192]{2,1,0:T(8,128)S(1)} %bitcast.12), channel_id=2, replica_groups=mesh['y'=4,'zh'=2,'core'=2,'xh'=2,'xl'=2,'zl'=8] {'core'}, dimensions={0}, use_global_device_ids=true | all-gather | bytes 1376256 | tf_op jit(solution)/shard_map/all_gather | solution.py:273
  9.0 0.1 pad_add_fusion.where
  9.1 0.0 collective-permute-done.passed_slots
  9.1 1.4 %lookup.1 = f32[8,8,256]{2,1,0:T(8,128)S(1)} custom-call(s32[3]{0:T(128)S(1)} %pad_add_fusion.where, s32[8,128]{1,0:T(8,128)S(1)} %slots.1.own_slots, s32[8,128]{1,0:T(8,128)S(1)} %collective-permute-done.passed_slots, f32[2,14,8192]{2,1,0:T(8,128)S(1)} %all-gather.2.tables), custom_call_target="tpu_custom_call" | custom-call | tf_op jit(solution)/shard_map/lookup/pallas_call | solution.py:274
  10.5 20.4 %all_to_all.10.received = f32[8,8,256]{2,1,0:T(8,128)S(1)} all-to-all(f32[8,8,256]{2,1,0:T(8,128)S(1)} %lookup.1), channel_id=1, replica_groups={{320,192,448,64,256,128,384,0},{321,193,449,65,257,129,385,1},{322,194,..., dimensions={0} | all-to-all | bytes 131072 | tf_op jit(solution)/shard_map/all_to_all | solution.py:283
  30.8 10.6 %forces.1 = f32[16,8,256]{2,1,0:T(8,128)} custom-call(f32[8,8,256]{2,1,0:T(8,128)S(1)} %all_to_all.10.received, f32[2,14,8192]{2,1,0:T(8,128)S(1)} %all-gather.2.tables), custom_call_target="tpu_custom_call" | custom-call | tf_op jit(solution)/shard_map/forces/pallas_call | solution.py:284
  41.5 0.0 copy-start.1
  41.5 6.5 %all-to-all-start.1 = ((f32[16,8,256]{2,1,0:T(8,128)}), f32[16,8,256]{2,1,0:T(8,128)S(1)}, u32[]{:S(2)}, u32[]{:S(2)}) async-start(f32[16,8,256]{2,1,0:T(8,128)} %forces.1), calls=%async_computation.1 | async-start | bytes 262144 | tf_op jit(solution)/shard_map/all_to_all | solution.py:294
  48.0 0.0 copy-done.1
  48.0 15.9 %all-to-all-done.1.received = f32[16,8,256]{2,1,0:T(8,128)S(1)} async-done(((f32[16,8,256]{2,1,0:T(8,128)}), f32[16,8,256]{2,1,0:T(8,128)S(1)}, u32[]{:S(2)}, u32[]{:S(2)}) %all-to-all-start.1) | async-done | bytes 131104 | tf_op jit(solution)/shard_map/all_to_all | solution.py:294
  63.8 0.1 corrector.1
  63.9 2.2 %all-gather.3 = f32[2,12,512]{2,1,0:T(8,128)S(1)} all-gather(f32[1,12,512]{2,1,0:T(8,128)S(1)} %bitcast.13), channel_id=3, replica_groups=mesh['y'=4,'zh'=2,'core'=2,'xh'=2,'xl'=2,'zl'=8] {'core'}, dimensions={0}, use_global_device_ids=true | all-gather | bytes 73728 | tf_op jit(solution)/shard_map/all_gather | solution.py:303
  66.2 0.6 maximum_select_fusion
  (3 shorter events, 0.0 us)
Async XLA Ops:
  0.0 0.7 %copy-start = (s32[1024]{0:T(1024)S(1)}, s32[1024]{0:T(1024)}, u32[]{:S(2)}) copy-start(s32[1024]{0:T(1024)} %param.7) | copy-start | bytes 12292
  0.7 4.5 %copy-start.2 = (f32[12,8192]{1,0:T(8,128)S(1)}, f32[12,8192]{1,0:T(8,128)}, u32[]{:S(2)}) copy-start(f32[12,8192]{1,0:T(8,128)} %state_in.1) | copy-start | bytes 1179652
  0.7 4.6 %copy-start.3 = (f32[8192]{0:T(1024)S(1)}, f32[8192]{0:T(1024)}, u32[]{:S(2)}) copy-start(f32[8192]{0:T(1024)} %param.5) | copy-start | bytes 98308
  0.7 4.6 %copy-start.4 = (s32[8192]{0:T(1024)S(1)}, s32[8192]{0:T(1024)}, u32[]{:S(2)}) copy-start(s32[8192]{0:T(1024)} %param.6) | copy-start | bytes 98308
  0.7 8.4 %collective-permute-start = (s32[8,128]{1,0:T(8,128)S(1)}, s32[8,128]{1,0:T(8,128)S(1)}, u32[]{:S(2)}, u32[]{:S(2)}) collective-permute-start(s32[8,128]{1,0:T(8,128)S(1)} %slots.1.own_slots), channel_id=1, source_target_pairs={{0,24},{8,16},{16,8},{24,0},{1,25},{9,17},{17,9},{25,1},{2,26},{10... | collective-permute-start | bytes 12296 | tf_op jit(solution)/shard_map/ppermute | solution.py:256
  41.5 6.5 %copy-start.1 = (s32[1024]{0:T(1024)S(1)}, s32[1024]{0:T(1024)}, u32[]{:S(2)}) copy-start(s32[1024]{0:T(1024)} %param.7) | copy-start | bytes 12292
  41.5 22.4 %all-to-all-start.1 = ((f32[16,8,256]{2,1,0:T(8,128)}), f32[16,8,256]{2,1,0:T(8,128)S(1)}, u32[]{:S(2)}, u32[]{:S(2)}) async-start(f32[16,8,256]{2,1,0:T(8,128)} %forces.1), calls=%async_computation.1 | async-start | bytes 262144 | tf_op jit(solution)/shard_map/all_to_all | solution.py:294
